TPU v7x, 32 devices: a whole 2x2x4 slice. The times are simulated.
32 devices in a mesh: dp: 8 (over z, x), tensor: 4 (over y, core).
Axes of the slice: x: 2, y: 2, z: 4, core: 2. Of those that a mesh axis runs over, the one named last changes fastest.
Arguments:
- hidden_in: bfloat16 [4, 4096, 1024], P(None, 'dp'), may hold values from -6 to 6
- cotangent: bfloat16 [4, 4096, 1024], P(None, 'dp'), may hold values from -6 to 6
- doc_lengths: int32 [4, 6], replicated, may hold values from 1 to 3584, as said below
- norm1_gain: float32 [1024], replicated, may hold values from 0.1 to 1.9
- norm1_bias: float32 [1024], replicated, may hold values from -1.75 to 1.75
- norm2_gain: float32 [1024], replicated, may hold values from 0.1 to 1.9
- norm2_bias: float32 [1024], replicated, may hold values from -1.75 to 1.75
- qkv_weight: bfloat16 [1024, 16, 192], P('dp', 'tensor'), may hold values from -0.1875 to 0.1875
- qkv_bias: float32 [16, 192], P('tensor'), may hold values from -1.75 to 1.75
- out_weight: bfloat16 [16, 64, 1024], P('tensor', None, 'dp'), may hold values from -1 to 1
- out_bias: float32 [1024], replicated, may hold values from -3 to 3
- fc1_weight: bfloat16 [1024, 4096], P('dp', 'tensor'), may hold values from -0.1875 to 0.1875
- fc1_bias: float32 [4096], P('tensor'), may hold values from -3 to 3
- fc2_weight: bfloat16 [4096, 1024], P('tensor', 'dp'), may hold values from -0.09375 to 0.09375
Outputs:
- layer_out: bfloat16 [4, 4096, 1024], P(None, 'dp')
- grad_input: bfloat16 [4, 4096, 1024], P(None, 'dp')
- grad_norm1_gain: float32 [1024], replicated
- grad_norm1_bias: float32 [1024], replicated
- grad_norm2_gain: float32 [1024], replicated
- grad_norm2_bias: float32 [1024], replicated
- grad_qkv_weight: float32 [1024, 16, 192], P('dp', 'tensor')
- grad_qkv_bias: float32 [16, 192], P('tensor')
- grad_out_weight: float32 [16, 64, 1024], P('tensor', None, 'dp')
- grad_out_bias: float32 [1024], replicated
- grad_fc1_weight: float32 [1024, 4096], P('dp', 'tensor')
- grad_fc1_bias: float32 [4096], P('tensor')
- grad_fc2_weight: float32 [4096, 1024], P('tensor', 'dp')
Inputs may be any that keep to these rules, and one draw needn't show every extreme that they name: `doc_lengths`: each row lists the lengths of the 6 documents packed in order into one sequence; each row sums to 4096. In every row but one, each document has 200 to min(2000, 3584) tokens; in one row, drawn from the seed, one document has exactly 3584 tokens and the others are short.
All inputs are finite; a program needn't handle non-finite values.
Results may differ from a plain program's by a relative error of at most 0.015.
Values may be sent and summed in bfloat16 or wider, within the bound.
A program may use at most 192 MiB of HBM per device.

v0:
```python
from functools import partial
import math

import jax
import jax.numpy as jnp
from jax import lax
from jax.sharding import PartitionSpec as P

HEAD = 64
ROT = 16


norm_epsilon = 1e-05
masked_score = -1e30


def documents(lengths, token_index):
    bounds = jnp.cumsum(lengths)
    passed = bounds[None, :] <= token_index[:, None]
    segment = jnp.sum(passed.astype(jnp.int32), axis=1)
    doc_start = jnp.max(jnp.where(passed, bounds[None, :], 0), axis=1)
    return (segment, token_index - doc_start)


def rotary_angles(position):
    half_width = ROT // 2
    frequency = jnp.power(10000.0, -2.0 * jnp.arange(half_width, dtype=jnp.float32) / ROT)
    angles = position.astype(jnp.float32)[..., None] * frequency
    return (jnp.cos(angles)[..., None, :], jnp.sin(angles)[..., None, :])


def rotary(vectors, cosine_table, sine_table):
    half_width = cosine_table.shape[-1]
    lower_half = vectors[..., :half_width]
    upper_half = vectors[..., half_width : 2 * half_width]
    return jnp.concatenate(
        [
            lower_half * cosine_table - upper_half * sine_table,
            upper_half * cosine_table + lower_half * sine_table,
            vectors[..., 2 * half_width :],
        ],
        axis=-1,
    )


def layer_norm(values, gain, bias):
    centered = values - jnp.mean(values, axis=-1, keepdims=True)
    variance = jnp.mean(centered * centered, axis=-1, keepdims=True)
    return centered * lax.rsqrt(variance + norm_epsilon) * gain + bias


def norm_pair(hidden, gain_one, bias_one, gain_two, bias_two):
    return (layer_norm(hidden, gain_one, bias_one), layer_norm(hidden, gain_two, bias_two))


def block_scores(
    queries, keys_rot, query_index, query_segment, key_index, key_segment, score_scale
):
    scores = (
        jnp.einsum("qhe,khe->hqk", queries, keys_rot, preferred_element_type=jnp.float32)
        * score_scale
    )
    allowed = (query_index[:, None] >= key_index[None, :]) & (
        query_segment[:, None] == key_segment[None, :]
    )
    return (scores, allowed)


def shards(
    hidden_in,
    cotangent,
    doc_lengths,
    norm1_gain,
    norm1_bias,
    norm2_gain,
    norm2_bias,
    qkv_weight,
    qkv_bias,
    out_weight,
    out_bias,
    fc1_weight,
    fc1_bias,
    fc2_weight,
):
    micro_count, tok_rows, model_width = hidden_in.shape
    head_count = qkv_bias.shape[0]
    hidden_units = fc1_bias.shape[0]
    dp_count = lax.axis_size("dp")
    seq_length = tok_rows * dp_count
    query_index = lax.axis_index("dp") * tok_rows + jnp.arange(tok_rows, dtype=jnp.int32)
    score_scale = HEAD ** (-0.5)
    group_shards = math.gcd(dp_count, max(1, 512 // tok_rows))
    block_rows = tok_rows * group_shards
    block_count = seq_length // block_rows
    weights_in = (qkv_weight, out_weight, fc1_weight, fc2_weight)
    grad_w_qkv = jnp.zeros((model_width, head_count, 3 * HEAD), jnp.float32)
    grad_w_out = jnp.zeros((head_count, HEAD, model_width), jnp.float32)
    grad_w_up = jnp.zeros((model_width, hidden_units), jnp.float32)
    grad_w_down = jnp.zeros((hidden_units, model_width), jnp.float32)
    grad_b_qkv = jnp.zeros((head_count, 3 * HEAD), jnp.float32)
    grad_b_up = jnp.zeros((hidden_units,), jnp.float32)
    grad_b_out = jnp.zeros((model_width,), jnp.float32)
    grad_norms = jnp.zeros((4, model_width), jnp.float32)
    outputs = []
    input_grads = []
    for micro_index in range(micro_count):
        w_qkv, w_out, w_up, w_down = (
            lax.all_gather(weights_in[0], "dp", axis=0, tiled=True),
            lax.all_gather(weights_in[1], "dp", axis=2, tiled=True),
            lax.all_gather(weights_in[2], "dp", axis=0, tiled=True),
            lax.all_gather(weights_in[3], "dp", axis=1, tiled=True),
        )
        lengths = doc_lengths[micro_index]
        query_segment, query_position = documents(lengths, query_index)
        cosine_table, sine_table = rotary_angles(query_position)
        hidden = hidden_in[micro_index].astype(jnp.float32)
        first_norm, second_norm = norm_pair(hidden, norm1_gain, norm1_bias, norm2_gain, norm2_bias)
        first_low = first_norm.astype(jnp.bfloat16)
        second_low = second_norm.astype(jnp.bfloat16)
        projected = (
            jnp.einsum("td,dhe->the", first_low, w_qkv, preferred_element_type=jnp.float32)
            + qkv_bias
        )
        queries = rotary(projected[..., :HEAD], cosine_table, sine_table).astype(jnp.bfloat16)
        keys_rot = rotary(projected[..., HEAD : 2 * HEAD], cosine_table, sine_table).astype(
            jnp.bfloat16
        )
        values = projected[..., 2 * HEAD :].astype(jnp.bfloat16)
        key_value = jnp.concatenate([keys_rot, values], axis=-1)
        key_piece = lax.all_gather(key_value, "dp", axis=0, tiled=True)
        key_index = jnp.arange(key_piece.shape[0], dtype=jnp.int32)
        key_segment, unused = documents(lengths, key_index)
        old_max = jnp.full((head_count, tok_rows), masked_score, jnp.float32)
        scores, allowed = block_scores(
            queries,
            key_piece[..., :HEAD],
            query_index,
            query_segment,
            key_index,
            key_segment,
            score_scale,
        )
        masked = jnp.where(allowed[None], scores, masked_score)
        new_max = jnp.maximum(old_max, jnp.max(masked, axis=-1))
        exponent = jnp.where(allowed[None], jnp.exp(masked - new_max[..., None]), 0.0)
        summed = jnp.sum(exponent, axis=-1)
        increment = jnp.einsum(
            "hqk,khe->hqe",
            exponent.astype(jnp.bfloat16),
            key_piece[..., HEAD:],
            preferred_element_type=jnp.float32,
        )
        attended = increment / summed[..., None]
        log_total = new_max + jnp.log(summed)
        attended_low = attended.astype(jnp.bfloat16)
        attn_part = jnp.einsum(
            "hte,hed->td", attended_low, w_out, preferred_element_type=jnp.float32
        )
        up_proj = jnp.dot(second_low, w_up, preferred_element_type=jnp.float32) + fc1_bias
        act_low = jax.nn.gelu(up_proj, approximate=False).astype(jnp.bfloat16)
        down_part = jnp.dot(act_low, w_down, preferred_element_type=jnp.float32)
        branches = lax.psum((attn_part + down_part).astype(jnp.bfloat16), "tensor").astype(
            jnp.float32
        )
        outputs.append((hidden + branches + out_bias).astype(jnp.bfloat16))
        grad_out = cotangent[micro_index].astype(jnp.float32)
        grad_low = grad_out.astype(jnp.bfloat16)
        w_qkv, w_out, w_up, w_down = (
            lax.all_gather(weights_in[0], "dp", axis=0, tiled=True),
            lax.all_gather(weights_in[1], "dp", axis=2, tiled=True),
            lax.all_gather(weights_in[2], "dp", axis=0, tiled=True),
            lax.all_gather(weights_in[3], "dp", axis=1, tiled=True),
        )
        grad_b_out = grad_b_out + jnp.sum(grad_out, axis=0)
        grad_act = jnp.einsum("td,fd->tf", grad_low, w_down, preferred_element_type=jnp.float32)
        grad_w_down = grad_w_down + jnp.einsum(
            "tf,td->fd", act_low, grad_low, preferred_element_type=jnp.float32
        )
        unused, gelu_pull = jax.vjp(partial(jax.nn.gelu, approximate=False), up_proj)
        grad_up_low = gelu_pull(grad_act)[0].astype(jnp.bfloat16)
        grad_b_up = grad_b_up + jnp.sum(grad_up_low.astype(jnp.float32), axis=0)
        grad_w_up = grad_w_up + jnp.einsum(
            "td,tf->df", second_low, grad_up_low, preferred_element_type=jnp.float32
        )
        grad_second = jnp.einsum("tf,df->td", grad_up_low, w_up, preferred_element_type=jnp.float32)
        grad_w_out = grad_w_out + jnp.einsum(
            "hte,td->hed", attended_low, grad_low, preferred_element_type=jnp.float32
        )
        grad_att_low = jnp.einsum(
            "td,hed->hte", grad_low, w_out, preferred_element_type=jnp.float32
        ).astype(jnp.bfloat16)
        row_delta = jnp.sum(grad_att_low.astype(jnp.float32) * attended, axis=-1)
        every_key = lax.all_gather(key_value, "dp", axis=0, tiled=True)

        def key_block(grad_queries, block_index):
            offset = block_index * block_rows
            key_piece = lax.dynamic_slice_in_dim(every_key, offset, block_rows, 0)
            key_index = offset + jnp.arange(block_rows, dtype=jnp.int32)
            key_segment, unused_pos = documents(lengths, key_index)
            scores, allowed = block_scores(
                queries,
                key_piece[..., :HEAD],
                query_index,
                query_segment,
                key_index,
                key_segment,
                score_scale,
            )
            attn_probs = jnp.where(allowed[None], jnp.exp(scores - log_total[..., None]), 0.0)
            grad_values = jnp.einsum(
                "hqk,hqe->khe",
                attn_probs.astype(jnp.bfloat16),
                grad_att_low,
                preferred_element_type=jnp.float32,
            )
            grad_probs = jnp.einsum(
                "hqe,khe->hqk",
                grad_att_low,
                key_piece[..., HEAD:],
                preferred_element_type=jnp.float32,
            )
            grad_scores = (attn_probs * (grad_probs - row_delta[..., None])).astype(jnp.bfloat16)
            new_accum = grad_queries + score_scale * jnp.einsum(
                "hqk,khe->qhe",
                grad_scores,
                key_piece[..., :HEAD],
                preferred_element_type=jnp.float32,
            )
            grad_keys = score_scale * jnp.einsum(
                "hqk,qhe->khe", grad_scores, queries, preferred_element_type=jnp.float32
            )
            return (new_accum, jnp.concatenate([grad_keys, grad_values], axis=-1))

        grad_queries, key_terms = lax.scan(
            key_block, jnp.zeros((tok_rows, head_count, HEAD), jnp.float32), jnp.arange(block_count)
        )
        key_terms = key_terms.reshape(seq_length, head_count, 2 * HEAD)
        own_terms = lax.psum_scatter(
            key_terms.astype(jnp.bfloat16), "dp", scatter_dimension=0, tiled=True
        ).astype(jnp.float32)
        grad_proj_low = jnp.concatenate(
            [
                rotary(grad_queries, cosine_table, -sine_table),
                rotary(own_terms[..., :HEAD], cosine_table, -sine_table),
                own_terms[..., HEAD:],
            ],
            axis=-1,
        ).astype(jnp.bfloat16)
        grad_b_qkv = grad_b_qkv + jnp.sum(grad_proj_low.astype(jnp.float32), axis=0)
        grad_w_qkv = grad_w_qkv + jnp.einsum(
            "td,the->dhe", first_low, grad_proj_low, preferred_element_type=jnp.float32
        )
        grad_first = jnp.einsum(
            "the,dhe->td", grad_proj_low, w_qkv, preferred_element_type=jnp.float32
        )
        unused_norms, norm_pull = jax.vjp(
            norm_pair, hidden, norm1_gain, norm1_bias, norm2_gain, norm2_bias
        )
        whole_first, whole_second = (
            lax.psum(grad_first.astype(jnp.bfloat16), "tensor").astype(jnp.float32),
            lax.psum(grad_second.astype(jnp.bfloat16), "tensor").astype(jnp.float32),
        )
        norm_hidden, gain_one_grad, bias_one_grad, gain_two_grad, bias_two_grad = norm_pull(
            (whole_first, whole_second)
        )
        grad_hidden = grad_out + norm_hidden
        grad_norms = grad_norms + jnp.stack(
            [gain_one_grad, bias_one_grad, gain_two_grad, bias_two_grad]
        )
        input_grads.append(grad_hidden.astype(jnp.bfloat16))
    small_sums = lax.psum((grad_b_out, grad_norms, grad_b_qkv, grad_b_up), "dp")
    weight_sums = (
        lax.psum_scatter(
            grad_w_qkv.astype(jnp.bfloat16), "dp", scatter_dimension=0, tiled=True
        ).astype(jnp.float32),
        lax.psum_scatter(
            grad_w_out.astype(jnp.bfloat16), "dp", scatter_dimension=2, tiled=True
        ).astype(jnp.float32),
        lax.psum_scatter(
            grad_w_up.astype(jnp.bfloat16), "dp", scatter_dimension=0, tiled=True
        ).astype(jnp.float32),
        lax.psum_scatter(
            grad_w_down.astype(jnp.bfloat16), "dp", scatter_dimension=1, tiled=True
        ).astype(jnp.float32),
    )
    norm_sums = small_sums[1]
    return (
        jnp.stack(outputs),
        jnp.stack(input_grads),
        norm_sums[0],
        norm_sums[1],
        norm_sums[2],
        norm_sums[3],
        weight_sums[0],
        small_sums[2],
        weight_sums[1],
        small_sums[0],
        weight_sums[2],
        small_sums[3],
        weight_sums[3],
    )


def solution(mesh):
    return jax.shard_map(
        shards,
        mesh=mesh,
        in_specs=(
            P(None, "dp", None),
            P(None, "dp", None),
            P(),
            P(),
            P(),
            P(),
            P(),
            P("dp", "tensor", None),
            P("tensor", None),
            P("tensor", None, "dp"),
            P(),
            P("dp", "tensor"),
            P("tensor"),
            P("tensor", "dp"),
        ),
        out_specs=(
            P(None, "dp", None),
            P(None, "dp", None),
            P(),
            P(),
            P(),
            P(),
            P("dp", "tensor", None),
            P("tensor", None),
            P("tensor", None, "dp"),
            P(),
            P("dp", "tensor"),
            P("tensor"),
            P("tensor", "dp"),
        ),
        check_vma=False,
    )
```

profile of v0, /device:TPU:0, one launch (start us, length us, event | category | flops | bytes accessed | tf_op | source)
XLA Modules:
  0.0 1720.5 jit_solution(1863270167288493147)
XLA Ops:
  15.7 42.4 %all-gather.8.cloned.1.call-done = bf16[1024,4,192]{0,2,1:T(8,128)(2,1)} async-done(((bf16[128,4,192]{0,2,1:T(8,128)(2,1)}), bf16[1024,4,192]{0,2,1:T(8,128)(2,1)}) %all-gather.8.cloned.1.call-update) | async-done | bytes 1572880 | tf_op jit(solution)/shard_map/all_gather | solution.py:108
  63.7 29.8 %all_gather.18 = bf16[4,64,1024]{2,1,0:T(8,128)(2,1)S(1)} all-gather(bf16[4,64,128]{2,1,0:T(8,128)(2,1)S(1)} %copy-done.108), channel_id=1, replica_groups=mesh['dp'=8,'tensor'=4] {'dp'}, dimensions={2}, use_global_device_ids=true | all-gather | bytes 589824 | tf_op jit(solution)/shard_map/all_gather | solution.py:109
  96.1 8.4 fusion.119
  105.5 36.9 %all-gather.16.cloned.1.call-done = bf16[4096,4,128]{0,2,1:T(8,128)(2,1)} async-done(((bf16[512,4,128]{0,2,1:T(8,128)(2,1)}), bf16[4096,4,128]{0,2,1:T(8,128)(2,1)}) %all-gather.16.cloned.1.call-update) | async-done | bytes 4194320 | tf_op jit(solution)/shard_map/all_gather | solution.py:130
  142.3 15.8 fusion.93
  158.1 15.9 fusion.98
  174.0 16.6 multiply_reduce_fusion.2
  193.1 115.7 %while.61 = (s32[]{:T(128)}, f32[512,4,64]{0,2,1:T(8,128)S(1)}, bf16[8,512,4,128]{1,3,2,0:T(8,128)(2,1)}, s32[8]{0:T(128)S(1)}, bf16[4096,4,128]{0,2,1:T(8,128)(...) while((s32[]{:T(128)}, f32[512,4,64]{0,2,1:T(8,128)S(1)}, ...), condition=%wide.region_55.56_spmd.clone, body=%wide.region_53.55_spmd.clone.sunk | while | flops 684074496 | bytes 41984860 | solution.py:234
  198.9 4.0 fusion.611
  213.3 4.0 fusion.611
  227.7 4.0 fusion.611
  242.1 4.0 fusion.611
  256.5 4.0 fusion.611
  270.9 4.0 fusion.611
  285.3 4.0 fusion.611
  299.8 4.0 fusion.611
  308.8 4.8 copy.96
  313.8 86.7 %reduce-scatter.17.cloned.1.call-done = bf16[512,4,128]{0,2,1:T(8,128)(2,1)} async-done(((bf16[4096,4,128]{0,2,1:T(8,128)(2,1)}), bf16[512,4,128]{0,2,1:T(8,128)(2,1)}) %reduce-scatter.17.cloned.1.call-update) | async-done | bytes 524304 | tf_op jit(solution)/shard_map/reduce_scatter | solution.py:238
  404.5 35.3 %all-reduce.5.cloned.1.call-done = bf16[512,1024]{1,0:T(8,128)(2,1)} async-done(((bf16[512,1024]{1,0:T(8,128)(2,1)}), bf16[512,1024]{1,0:T(8,128)(2,1)}) %all-reduce.5.cloned.1.call-update) | async-done | bytes 1048592 | tf_op jit(solution)/shard_map/psum | solution.py:260
  464.2 27.3 %all-gather.12.cloned.1.call-done = bf16[1024,1024]{1,0:T(8,128)(2,1)} async-done(((bf16[128,1024]{1,0:T(8,128)(2,1)}), bf16[1024,1024]{1,0:T(8,128)(2,1)}) %all-gather.12.cloned.1.call-update) | async-done | bytes 2097168 | tf_op jit(solution)/shard_map/all_gather | solution.py:110
  491.5 4.5 fusion.396
  500.5 66.4 %all-gather.10.cloned.1.call-done = bf16[4096,4,128]{0,2,1:T(8,128)(2,1)} async-done(((bf16[512,4,128]{0,2,1:T(8,128)(2,1)}), bf16[4096,4,128]{0,2,1:T(8,128)(2,1)}) %all-gather.10.cloned.1.call-update) | async-done | bytes 4194320 | tf_op jit(solution)/shard_map/all_gather | solution.py:130
  566.9 16.1 fusion.92
  583.1 16.0 fusion.96
  599.1 16.9 multiply_reduce_fusion.3
  618.5 116.7 %while.60 = (s32[]{:T(128)}, f32[512,4,64]{0,2,1:T(8,128)}, bf16[8,512,4,128]{1,3,2,0:T(8,128)(2,1)}, s32[8]{0:T(128)S(1)}, bf16[4096,4,128]{0,2,1:T(8,128)(2,1)...) while((s32[]{:T(128)}, f32[512,4,64]{0,2,1:T(8,128)}, ...), condition=%wide.region_43.44_spmd.clone, body=%wide.region_41.43_spmd.clone.sunk | while | flops 684074496 | bytes 41984852 | solution.py:234
  624.1 4.0 fusion.595
  638.5 4.0 fusion.595
  653.0 4.0 fusion.595
  667.6 4.0 fusion.595
  682.2 4.0 fusion.595
  696.8 4.0 fusion.595
  711.4 4.0 fusion.595
  725.9 4.1 fusion.595
  735.2 15.8 fusion.94
  751.0 5.0 copy.95
  756.0 15.6 fusion.100
  772.6 16.4 multiply_reduce_fusion.1
  791.5 106.9 %while.62 = (s32[]{:T(128)}, f32[512,4,64]{0,2,1:T(8,128)S(1)}, bf16[8,512,4,128]{1,3,2,0:T(8,128)(2,1)}, s32[8]{0:T(128)S(1)}, bf16[4096,4,128]{0,2,1:T(8,128)(...) while((s32[]{:T(128)}, f32[512,4,64]{0,2,1:T(8,128)S(1)}, ...), condition=%wide.region_67.68_spmd.clone, body=%wide.region_65.67_spmd.clone.sunk | while | flops 684074496 | bytes 40936248 | solution.py:234
  796.8 4.0 fusion.627
  823.6 4.0 fusion.627
  898.5 5.0 copy.97
  903.5 15.8 fusion.95
  919.3 15.7 fusion.102
  936.0 16.0 multiply_reduce_fusion
  954.5 107.0 %while.63 = (s32[]{:T(128)}, f32[512,4,64]{0,2,1:T(8,128)S(1)}, bf16[8,512,4,128]{1,3,2,0:T(8,128)(2,1)}, s32[8]{0:T(128)S(1)}, bf16[4096,4,128]{0,2,1:T(8,128)(...) while((s32[]{:T(128)}, f32[512,4,64]{0,2,1:T(8,128)S(1)}, ...), condition=%wide.region_79.80_spmd.clone, body=%wide.region_77.79_spmd.clone.sunk | while | flops 684074496 | bytes 40936248 | solution.py:234
  959.8 4.0 fusion.643
  973.2 4.0 fusion.643
  986.6 4.0 fusion.643
  1000.0 4.2 fusion.643
  1061.5 4.7 copy.98
  1067.5 4.2 fusion.410
  1075.5 22.7 %multiply_convert_fusion.3 = (bf16[512,1024]{1,0:T(8,128)(2,1)S(1)}, f32[512,1024]{1,0:T(8,128)}, bf16[512,1024]{1,0:T(8,128)(2,1)S(1)}, f32[512,1024]{1,0:T(8,1...) fusion(f32[1024]{0:T(1024)S(1)} %copy-done.141, ...), kind=kOutput, calls=%fused_computation.377 | convolution fusion | flops 1215299584 | bytes 24133632 | tf_op jit(solution)/shard_map/dot_general | solution.py:159
  1107.0 5.4 convert_reduce_fusion.23
  1134.6 4.3 fusion.428
  1158.4 4.1 fusion.414
  1163.9 4.0 fusion.406
  1202.4 22.3 %reduce-scatter.29.cloned.1.call-done = bf16[128,1024]{1,0:T(8,128)(2,1)} async-done(((bf16[1024,1024]{1,0:T(8,128)(2,1)}), bf16[128,1024]{1,0:T(8,128)(2,1)}) %reduce-scatter.29.cloned.1.call-update) | async-done | bytes 262160
  1226.7 68.6 %reduce-scatter.23.cloned.1.call-done = bf16[128,1024]{1,0:T(8,128)(2,1)} async-done(((bf16[1024,1024]{1,0:T(8,128)(2,1)}), bf16[128,1024]{1,0:T(8,128)(2,1)}) %reduce-scatter.23.cloned.1.call-update) | async-done | bytes 262160 | tf_op jit(solution)/shard_map/reduce_scatter | solution.py:279
  1297.1 62.6 %reduce-scatter.27.cloned.1.call-done = bf16[128,256]{1,0:T(8,128)(2,1)} async-done(((bf16[1024,256]{1,0:T(8,128)(2,1)}), bf16[128,256]{1,0:T(8,128)(2,1)}) %reduce-scatter.27.cloned.1.call-update) | async-done | bytes 65552
  1363.3 64.2 %reduce-scatter.25.cloned.1.call-done = bf16[128,768]{1,0:T(8,128)(2,1)} async-done(((bf16[1024,768]{1,0:T(8,128)(2,1)}), bf16[128,768]{1,0:T(8,128)(2,1)}) %reduce-scatter.25.cloned.1.call-update) | async-done | bytes 196624
  1429.4 208.9 %all-reduce.7.cloned.1.call-done = (bf16[512,1024]{1,0:T(8,128)(2,1)}, bf16[512,1024]{1,0:T(8,128)(2,1)}, bf16[512,1024]{1,0:T(8,128)(2,1)}, bf16[512,1024]{1,0:...) async-done(((bf16[512,1024]{1,0:T(8,128)(2,1)}, ...) | async-done | bytes 11534352 | tf_op jit(solution)/shard_map/psum | solution.py:162
  1638.3 6.0 fusion.215
  1657.3 38.1 %all-reduce = (f32[4,1024]{1,0:T(4,128)S(1)}, f32[4,192]{1,0:T(4,128)}, f32[1024]{0:T(1024)}, f32[1024]{0:T(1024)}) all-reduce(f32[4,1024]{1,0:T(4,128)S(1)} %fusion.366, f32[4,192]{1,0:T(4,128)S(1)} %add_add_fusion.10, f32[1024]{0:T(1024)S(1)} %add_add_fusion.9, ...), channel_id=1, replica_groups=mesh['dp'=8,'tensor'=4] {'dp'}, use_global_device_ids=true, to_apply=%region_100.101 | all-reduce | flops 6912 | bytes 55296 | tf_op jit(solution)/shard_map/psum | solution.py:271
  (937 shorter events, 527.0 us)
Async XLA Ops:
  7.2 50.9 %all-gather.8.cloned.1.call-start = ((), (), s32[]{:S(2)}) async-start(), calls=%async_computation.8 | async-start | bytes 1769472 | tf_op jit(solution)/shard_map/all_gather | solution.py:108
  7.9 134.4 %all-gather.16.cloned.1.call-start = ((), (), s32[]{:S(2)}) async-start(), calls=%async_computation.12 | async-start | bytes 4718592 | tf_op jit(solution)/shard_map/all_gather | solution.py:130
  9.7 86.4 %copy-start.98 = (s32[512]{0:T(512)}, s32[512]{0:T(512)S(1)}, u32[]{:S(2)}) copy-start(s32[512]{0:T(512)S(1)} %get-tuple-element.1528) | copy-start | bytes 6148
  9.7 86.4 %copy-start.100 = (s32[512]{0:T(512)}, s32[512]{0:T(512)S(1)}, u32[]{:S(2)}) copy-start(s32[512]{0:T(512)S(1)} %get-tuple-element.1477) | copy-start | bytes 6148
  9.7 86.4 %copy-start.102 = (s32[512]{0:T(512)}, s32[512]{0:T(512)S(1)}, u32[]{:S(2)}) copy-start(s32[512]{0:T(512)S(1)} %get-tuple-element.1426) | copy-start | bytes 6148
  9.7 48.4 %copy-start.88 = (f32[1024]{0:T(1024)S(1)}, f32[1024]{0:T(1024)}, u32[]{:S(2)}) copy-start(f32[1024]{0:T(1024)} %param.25) | copy-start | bytes 12292
  9.7 48.4 %copy-start.142 = (f32[1024]{0:T(1024)S(1)}, f32[1024]{0:T(1024)}, u32[]{:S(2)}) copy-start(f32[1024]{0:T(1024)} %param.26) | copy-start | bytes 12292
  12.5 478.9 %copy-start.106 = (f32[512]{0:T(512)}, f32[512]{0:T(512)S(1)}, u32[]{:S(2)}) copy-start(f32[512]{0:T(512)S(1)} %broadcast_multiply_fusion.2) | copy-start | bytes 6148
  14.2 477.3 %copy-start.115 = (f32[512]{0:T(512)}, f32[512]{0:T(512)S(1)}, u32[]{:S(2)}) copy-start(f32[512]{0:T(512)S(1)} %fusion.372) | copy-start | bytes 6148
  15.7 435.0 %copy-start.70 = (f32[512,8]{0,1:T(8,128)}, f32[512,8]{0,1:T(8,128)S(1)}, u32[]{:S(2)}) copy-start(f32[512,8]{0,1:T(8,128)S(1)} %get-tuple-element.1016) | copy-start | bytes 49156
  15.7 436.0 %copy-start.68 = (f32[512,8]{0,1:T(8,128)}, f32[512,8]{0,1:T(8,128)S(1)}, u32[]{:S(2)}) copy-start(f32[512,8]{0,1:T(8,128)S(1)} %get-tuple-element.1011) | copy-start | bytes 49156
  15.7 438.0 %copy-start.66 = (f32[512,8]{0,1:T(8,128)}, f32[512,8]{0,1:T(8,128)S(1)}, u32[]{:S(2)}) copy-start(f32[512,8]{0,1:T(8,128)S(1)} %get-tuple-element.981) | copy-start | bytes 49156
  63.1 337.4 %reduce-scatter.17.cloned.1.call-start = ((), (), s32[]{:S(2)}) async-start(), calls=%async_computation.16 | async-start | bytes 4718592 | tf_op jit(solution)/shard_map/reduce_scatter | solution.py:238
  158.1 15.9 copy-start.43
  158.1 15.9 copy-start.149
  313.7 88.1 %copy-start.139 = (bf16[1024,4,192]{0,2,1:T(8,128)(2,1)S(1)}, bf16[1024,4,192]{0,2,1:T(8,128)(2,1)}, u32[]{:S(2)}) copy-start(bf16[1024,4,192]{0,2,1:T(8,128)(2,1)} %all-gather.8.cloned.1.call-done) | copy-start | bytes 4718596
  313.7 126.1 %all-reduce.5.cloned.1.call-start = ((), (), s32[]{:S(2)}) async-start(), calls=%async_computation.17 | async-start | bytes 2097152 | tf_op jit(solution)/shard_map/psum | solution.py:260
  403.8 87.7 %all-gather.12.cloned.1.call-start = ((), (), s32[]{:S(2)}) async-start(), calls=%async_computation.10 | async-start | bytes 2359296 | tf_op jit(solution)/shard_map/all_gather | solution.py:110
  404.4 162.5 %all-gather.10.cloned.1.call-start = ((), (), s32[]{:S(2)}) async-start(), calls=%async_computation.9 | async-start | bytes 4718592 | tf_op jit(solution)/shard_map/all_gather | solution.py:130
  404.5 42.4 %copy-start.94 = (f32[512]{0:T(512)}, f32[512]{0:T(512)S(1)}, u32[]{:S(2)}) copy-start(f32[512]{0:T(512)S(1)} %broadcast_multiply_fusion.3) | copy-start | bytes 6148
  404.5 39.9 %copy-start.104 = (f32[512]{0:T(512)}, f32[512]{0:T(512)S(1)}, u32[]{:S(2)}) copy-start(f32[512]{0:T(512)S(1)} %get-tuple-element.1045) | copy-start | bytes 6148
  404.5 41.1 %copy-start.96 = (f32[512]{0:T(512)}, f32[512]{0:T(512)S(1)}, u32[]{:S(2)}) copy-start(f32[512]{0:T(512)S(1)} %get-tuple-element.1044) | copy-start | bytes 6148
  451.6 283.6 %all-gather.18.cloned.1.call-start = ((), (), s32[]{:S(2)}) async-start(), calls=%async_computation.13 | async-start | bytes 4718592 | tf_op jit(solution)/shard_map/all_gather | solution.py:130
  453.6 449.9 %all-gather.20.cloned.1.call-start = ((), (), s32[]{:S(2)}) async-start(), calls=%async_computation.14 | async-start | bytes 4718592 | tf_op jit(solution)/shard_map/all_gather | solution.py:130
  453.8 45.4 %copy-start.90 = (bf16[512,4,8]{0,2,1:T(8,128)(2,1)}, bf16[512,4,8]{0,2,1:T(8,128)(2,1)S(1)}, u32[]{:S(2)}) copy-start(bf16[512,4,8]{0,2,1:T(8,128)(2,1)S(1)} %get-tuple-element.958) | copy-start | bytes 98308
  453.8 45.4 %copy-start.92 = (bf16[512,4,8]{0,2,1:T(8,128)(2,1)}, bf16[512,4,8]{0,2,1:T(8,128)(2,1)S(1)}, u32[]{:S(2)}) copy-start(bf16[512,4,8]{0,2,1:T(8,128)(2,1)S(1)} %get-tuple-element.961) | copy-start | bytes 98308
  454.6 652.3 %all-gather.14.cloned.1.call-start = ((), (), s32[]{:S(2)}) async-start(), calls=%async_computation.11 | async-start | bytes 2359296 | tf_op jit(solution)/shard_map/all_gather | solution.py:111
  455.4 701.7 %reduce-scatter.15.cloned.1.call-start = ((), (), s32[]{:S(2)}) async-start(), calls=%async_computation.15 | async-start | bytes 4718592 | tf_op jit(solution)/shard_map/reduce_scatter | solution.py:238
  458.2 33.3 %copy-start.78 = (f32[1024]{0:T(1024)S(1)}, f32[1024]{0:T(1024)}, u32[]{:S(2)}) copy-start(f32[1024]{0:T(1024)} %param.27) | copy-start | bytes 12292
  458.2 33.3 %copy-start.128 = (f32[1024]{0:T(1024)S(1)}, f32[1024]{0:T(1024)}, u32[]{:S(2)}) copy-start(f32[1024]{0:T(1024)} %param.28) | copy-start | bytes 12292
  496.0 70.9 %copy-start.30 = (pred[512,4096]{1,0:T(8,128)(4,1)S(1)}, pred[512,4096]{1,0:T(8,128)(4,1)}, u32[]{:S(2)}) copy-start(pred[512,4096]{1,0:T(8,128)(4,1)} %get-tuple-element.1006) | copy-start | bytes 6291460
  583.1 16.0 copy-start.42
  583.1 16.0 copy-start.147
  682.2 4.8 copy-start.6
  725.9 4.8 copy-start.6
  751.0 5.0 copy-start.29
  771.7 390.8 %reduce-scatter.19.cloned.1.call-start = ((), (), s32[]{:S(2)}) async-start(), calls=%async_computation.18 | async-start | bytes 4718592 | tf_op jit(solution)/shard_map/reduce_scatter | solution.py:238
  796.8 4.8 copy-start.7
  823.6 4.8 copy-start.7
  898.4 5.0 copy-start.15
  898.4 5.0 copy-start.28
  898.4 5.0 copy-start.64
  898.5 5.0 copy-start.91
  898.5 5.0 copy-start.93
  935.1 232.8 %reduce-scatter.21.cloned.1.call-start = ((), (), s32[]{:S(2)}) async-start(), calls=%async_computation.19 | async-start | bytes 4718592 | tf_op jit(solution)/shard_map/reduce_scatter | solution.py:238
  959.8 4.8 copy-start.8
  973.2 4.8 copy-start.8
  986.6 4.8 copy-start.8
  1000.0 5.0 copy-start.8
  1066.3 158.4 %reduce-scatter.29.cloned.1.call-start = ((), (), s32[]{:S(2)}) async-start(), calls=%async_computation.23 | async-start | bytes 2359296
  1075.5 22.7 %copy-start.155 = (f32[512,1024]{1,0:T(8,128)}, f32[512,1024]{1,0:T(8,128)S(1)}, u32[]{:S(2)}) copy-start(f32[512,1024]{1,0:T(8,128)S(1)} %fusion.388) | copy-start | bytes 6291460
  1075.5 22.7 %copy-start.9 = (bf16[4,512,1024]{2,1,0:T(8,128)(2,1)S(1)}, bf16[4,512,1024]{2,1,0:T(8,128)(2,1)}, u32[]{:S(2)}) copy-start(bf16[4,512,1024]{2,1,0:T(8,128)(2,1)} %param.23) | copy-start | bytes 12582916
  1106.5 188.8 %reduce-scatter.23.cloned.1.call-start = ((), (), s32[]{:S(2)}) async-start(), calls=%async_computation.20 | async-start | bytes 2359296 | tf_op jit(solution)/shard_map/reduce_scatter | solution.py:279
  1107.0 5.4 copy-start.2
  1133.4 226.3 %reduce-scatter.27.cloned.1.call-start = ((), (), s32[]{:S(2)}) async-start(), calls=%async_computation.22 | async-start | bytes 589824
  1157.0 270.5 %reduce-scatter.25.cloned.1.call-start = ((), (), s32[]{:S(2)}) async-start(), calls=%async_computation.21 | async-start | bytes 1769472
  1158.4 5.3 copy-start.62
  1179.3 459.0 %all-reduce.7.cloned.1.call-start = ((), (), s32[]{:S(2)}) async-start(), calls=%async_computation.24 | async-start | bytes 23068672 | tf_op jit(solution)/shard_map/psum | solution.py:162
  1297.1 341.2 %copy-start.26 = (bf16[512,1024]{1,0:T(8,128)(2,1)S(1)}, bf16[512,1024]{1,0:T(8,128)(2,1)}, u32[]{:S(2)}) copy-start(bf16[512,1024]{1,0:T(8,128)(2,1)} %all-reduce.5.cloned.1.call-done) | copy-start | bytes 3145732
  1638.3 6.0 copy-start.3
  1638.3 6.0 copy-start.19
  1638.3 6.0 copy-start.21
  1638.3 6.0 copy-start.23
  1638.3 6.0 copy-start.25
  (161 other events, 415.9 us)
Sparse Core Ops, SparseCore 0:
  10.1 47.9 all-gather.7
  63.2 79.0 all-gather.15
  313.8 86.6 reduce-scatter.16
  403.9 35.8 all-reduce.4
  441.8 49.6 all-gather.11
  493.4 73.4 all-gather.9
  569.0 73.1 all-gather.17
  644.8 73.2 all-gather.19
  720.1 49.2 all-gather.13
  773.5 86.4 reduce-scatter.14
  935.2 86.9 reduce-scatter.18
  1066.4 86.6 reduce-scatter.20
  1157.1 67.6 reduce-scatter.28
  1228.6 66.6 reduce-scatter.22
  1298.8 60.8 reduce-scatter.26
  1363.6 63.8 reduce-scatter.24
  1432.0 206.2 all-reduce.6
where the time goes:
time: 1730 us; the launch traced here: 1720 us
  waiting for transfers between devices  724 us (42%)
  matrix products  619 us (36%)
  other arithmetic  181 us (10%)
  local copies, waits for them, and re-layouts  87.6 us (5%)
  blocking collectives  67.9 us (4%)
  loops' own time  23.3 us (1%)
    psum x1, waiting for transfers between devices, shards(): lax.psum((attn_part + down_part).astype(jnp.bfloat16), 'tensor')  209 us
    dot_general x36, matrix products, block_scores(): jnp.einsum('qhe,khe->hqk', queries, keys_rot, preferred_element_type=jnp....  181 us
    unnamed x20, waiting for transfers between devices  151 us
    dot_general x32, matrix products, key_block(): jnp.einsum('hqe,khe->hqk', grad_att_low, key_piece[..., HEAD:], preferred...  128 us
    all_gather x4, waiting for transfers between devices, shards(): key_piece = lax.all_gather(key_value, 'dp', axis=0, tiled=True)  103 us
    reduce_scatter x4, waiting for transfers between devices, shards(): lax.psum_scatter(key_terms.astype(jnp.bfloat16), 'dp', scatter_dimension=...  86.7 us
    reduce_scatter x1, waiting for transfers between devices, shards(): lax.psum_scatter(grad_w_up.astype(jnp.bfloat16), 'dp', scatter_dimension=...  68.6 us
    dot_general x4, matrix products, shards(): jnp.einsum('hqk,khe->hqe', exponent.astype(jnp.bfloat16), key_piece[...,...  65.9 us
  transfers between devices with their start and end apart: 17, of which 11 were waited for; matrix products, arithmetic and copies ran while one was open for 38% of the time, Pallas kernels for 0%

commit v1 on v0

v1 whole, which is shorter than its diff:
```python
from functools import partial
import math

import jax
import jax.numpy as jnp
from jax import lax
from jax.experimental import pallas as pl
from jax.experimental.pallas import tpu as pltpu
from jax.sharding import PartitionSpec as P

HEAD = 64
ROT = 16


norm_epsilon = 1e-05
masked_score = -1e30


def documents(lengths, token_index):
    bounds = jnp.cumsum(lengths)
    passed = bounds[None, :] <= token_index[:, None]
    segment = jnp.sum(passed.astype(jnp.int32), axis=1)
    doc_start = jnp.max(jnp.where(passed, bounds[None, :], 0), axis=1)
    return (segment, token_index - doc_start)


def rotary_angles(position):
    half_width = ROT // 2
    frequency = jnp.power(10000.0, -2.0 * jnp.arange(half_width, dtype=jnp.float32) / ROT)
    angles = position.astype(jnp.float32)[..., None] * frequency
    return (jnp.cos(angles)[..., None, :], jnp.sin(angles)[..., None, :])


def rotary(vectors, cosine_table, sine_table):
    half_width = cosine_table.shape[-1]
    lower_half = vectors[..., :half_width]
    upper_half = vectors[..., half_width : 2 * half_width]
    return jnp.concatenate(
        [
            lower_half * cosine_table - upper_half * sine_table,
            upper_half * cosine_table + lower_half * sine_table,
            vectors[..., 2 * half_width :],
        ],
        axis=-1,
    )


NT = (((1,), (1,)), ((), ()))
TN = (((0,), (0,)), ((), ()))
NN = (((1,), (0,)), ((), ()))
score_scale = HEAD**-0.5
vmem_bytes = 44 * 1024 * 1024


def mul(a, b, dims):
    return lax.dot_general(a, b, dims, preferred_element_type=jnp.float32)


def attend_kernel(rows, first_ref, x_ref, start_ref, out_ref, lse_ref, delta_ref):
    unit, block = pl.program_id(0), pl.program_id(1)
    own = x_ref[0, pl.ds(pl.multiple_of(block * rows, rows), rows), :]
    queries = own[:, :HEAD] * jnp.bfloat16(score_scale)
    grad_att = own[:, 3 * HEAD :]
    query_index = block * rows + lax.broadcasted_iota(jnp.int32, (1, rows), 1)
    start = start_ref[0]

    def step(key_block, carry):
        top, total, acc = carry
        piece = x_ref[0, pl.ds(pl.multiple_of(key_block * rows, rows), rows), :]
        scores = mul(piece[:, HEAD : 2 * HEAD], queries, NT)
        key_index = key_block * rows + lax.broadcasted_iota(jnp.int32, (rows, rows), 0)
        allowed = (key_index <= query_index) & (key_index >= start)
        scores = jnp.where(allowed, scores, masked_score)
        new_top = jnp.maximum(top, jnp.max(scores, axis=0, keepdims=True))
        decay = jnp.exp(top - new_top)
        exponent = jnp.exp(scores - new_top)
        total = total * decay + jnp.sum(exponent, axis=0, keepdims=True)
        acc = acc * decay + mul(
            piece[:, 2 * HEAD : 3 * HEAD], exponent.astype(jnp.bfloat16), TN
        )
        return (new_top, total, acc)

    top, total, acc = lax.fori_loop(
        first_ref[unit, block],
        block + 1,
        step,
        (
            jnp.full((1, rows), masked_score, jnp.float32),
            jnp.zeros((1, rows), jnp.float32),
            jnp.zeros((HEAD, rows), jnp.float32),
        ),
    )
    attended = acc / total
    lse_ref[0] = top + jnp.log(total)
    delta_ref[0] = jnp.sum(attended * grad_att.astype(jnp.float32).T, axis=0, keepdims=True)
    out_ref[0] = attended.T.astype(jnp.bfloat16)


def attend_back_kernel(rows, last_ref, x_ref, start_ref, lse_ref, delta_ref, grad_ref, grad_q):
    unit, block = pl.program_id(0), pl.program_id(1)
    here = pl.ds(pl.multiple_of(block * rows, rows), rows)
    own = x_ref[0, here, :]
    keys, values = own[:, HEAD : 2 * HEAD], own[:, 2 * HEAD : 3 * HEAD]
    key_index = block * rows + lax.broadcasted_iota(jnp.int32, (rows, rows), 0)

    @pl.when(block == 0)
    def _():
        grad_q[...] = jnp.zeros_like(grad_q)

    def step(query_block, carry):
        grad_keys, grad_values = carry
        there = pl.ds(pl.multiple_of(query_block * rows, rows), rows)
        piece = x_ref[0, there, :]
        queries = piece[:, :HEAD] * jnp.bfloat16(score_scale)
        grad_att = piece[:, 3 * HEAD :]
        query_index = query_block * rows + lax.broadcasted_iota(jnp.int32, (1, rows), 1)
        allowed = (key_index <= query_index) & (key_index >= start_ref[0, :, there])
        scores = mul(keys, queries, NT)
        probs = jnp.where(allowed, jnp.exp(scores - lse_ref[0, :, there]), 0.0)
        grad_values = grad_values + mul(probs.astype(jnp.bfloat16), grad_att, NN)
        grad_probs = mul(values, grad_att, NT)
        grad_scores = (probs * (grad_probs - delta_ref[0, :, there])).astype(jnp.bfloat16)
        grad_keys = grad_keys + mul(grad_scores, queries, NN)
        grad_q[there, :] += mul(grad_scores, keys, TN)
        return (grad_keys, grad_values)

    zero = jnp.zeros((rows, HEAD), jnp.float32)
    grad_keys, grad_values = lax.fori_loop(block, last_ref[unit, block] + 1, step, (zero, zero))
    grad_ref[0, here, HEAD : 2 * HEAD] = grad_keys.astype(jnp.bfloat16)
    grad_ref[0, here, 2 * HEAD :] = grad_values.astype(jnp.bfloat16)

    @pl.when(block == pl.num_programs(1) - 1)
    def _():
        grad_ref[0, :, :HEAD] = (grad_q[...] * score_scale).astype(jnp.bfloat16)


def attention(packed, lengths):
    units, length, width = packed.shape
    rows = math.gcd(length, 512)
    blocks = length // rows
    bounds = jnp.cumsum(lengths, axis=1)[:, None, :]
    token = jnp.arange(length, dtype=jnp.int32)[None, :, None]
    start = jnp.max(jnp.where(bounds <= token, bounds, 0), axis=2)
    end = jnp.min(jnp.where(bounds > token, bounds, length), axis=2)
    first = start[:, ::rows] // rows
    last = (end[:, rows - 1 :: rows] - 1) // rows
    start = start[:, None, :]
    whole = pl.BlockSpec((1, length, width), lambda u, b, s: (u, 0, 0))
    line = pl.BlockSpec((1, 1, rows), lambda u, b, s: (u, 0, b))
    full_line = pl.BlockSpec((1, 1, length), lambda u, b, s: (u, 0, 0))
    pairs = units * length * length // 4
    out, lse, delta = pl.pallas_call(
        partial(attend_kernel, rows),
        grid_spec=pltpu.PrefetchScalarGridSpec(
            num_scalar_prefetch=1,
            grid=(units, blocks),
            in_specs=[whole, line],
            out_specs=[pl.BlockSpec((1, rows, HEAD), lambda u, b, s: (u, b, 0)), line, line],
        ),
        out_shape=[
            jax.ShapeDtypeStruct((units, length, HEAD), jnp.bfloat16),
            jax.ShapeDtypeStruct((units, 1, length), jnp.float32),
            jax.ShapeDtypeStruct((units, 1, length), jnp.float32),
        ],
        compiler_params=pltpu.CompilerParams(vmem_limit_bytes=vmem_bytes),
        cost_estimate=pl.CostEstimate(
            flops=pairs * 4 * 256, bytes_accessed=units * length * 700, transcendentals=pairs
        ),
    )(first, packed, start)
    grads = pl.pallas_call(
        partial(attend_back_kernel, rows),
        grid_spec=pltpu.PrefetchScalarGridSpec(
            num_scalar_prefetch=1,
            grid=(units, blocks),
            in_specs=[whole, full_line, full_line, full_line],
            out_specs=pl.BlockSpec((1, length, 3 * HEAD), lambda u, b, s: (u, 0, 0)),
            scratch_shapes=[pltpu.VMEM((length, HEAD), jnp.float32)],
        ),
        out_shape=jax.ShapeDtypeStruct((units, length, 3 * HEAD), jnp.bfloat16),
        compiler_params=pltpu.CompilerParams(vmem_limit_bytes=vmem_bytes),
        cost_estimate=pl.CostEstimate(
            flops=pairs * 10 * 256, bytes_accessed=units * length * 1000, transcendentals=pairs
        ),
    )(last, packed, start, lse, delta)
    return (out, grads)


def shards(
    hidden_in,
    cotangent,
    doc_lengths,
    norm1_gain,
    norm1_bias,
    norm2_gain,
    norm2_bias,
    qkv_weight,
    qkv_bias,
    out_weight,
    out_bias,
    fc1_weight,
    fc1_bias,
    fc2_weight,
):
    micros, tok_rows, width = hidden_in.shape
    heads = qkv_bias.shape[0]
    hidden_units = fc1_bias.shape[0]
    shard_rows = qkv_weight.shape[0]
    dp_count = lax.axis_size("dp")
    tokens = micros * tok_rows
    qkv_wide, att_wide = heads * 3 * HEAD, heads * HEAD
    unit_count = micros * heads
    units = -(-unit_count // dp_count)

    att_weights = lax.all_gather(
        jnp.concatenate(
            [qkv_weight.reshape(shard_rows, qkv_wide), out_weight.reshape(att_wide, shard_rows).T],
            axis=1,
        ),
        "dp",
        axis=0,
        tiled=True,
    )
    w_qkv, w_out = att_weights[:, :qkv_wide], att_weights[:, qkv_wide:]
    ff_weights = lax.all_gather(
        jnp.concatenate([fc1_weight, fc2_weight.T], axis=1), "dp", axis=0, tiled=True
    )
    w_up, w_down = ff_weights[:, :hidden_units], ff_weights[:, hidden_units:]

    query_index = lax.axis_index("dp") * tok_rows + jnp.arange(tok_rows, dtype=jnp.int32)
    position = jax.vmap(lambda lengths: documents(lengths, query_index)[1])(doc_lengths)
    cosine_table, sine_table = rotary_angles(position.reshape(tokens))
    hidden = hidden_in.reshape(tokens, width).astype(jnp.float32)
    grad_low = cotangent.reshape(tokens, width)
    centered = hidden - jnp.mean(hidden, axis=-1, keepdims=True)
    variance = jnp.mean(centered * centered, axis=-1, keepdims=True)
    inverse = lax.rsqrt(variance + norm_epsilon)
    unit_norm = centered * inverse
    first_low = (unit_norm * norm1_gain + norm1_bias).astype(jnp.bfloat16)
    second_low = (unit_norm * norm2_gain + norm2_bias).astype(jnp.bfloat16)

    def to_units(array):
        wide = array.shape[-1]
        array = array.reshape(micros, tok_rows, heads, wide).transpose(2, 0, 1, 3)
        array = array.reshape(unit_count, tok_rows, wide)
        array = jnp.pad(array, ((0, units * dp_count - unit_count), (0, 0), (0, 0)))
        return lax.all_to_all(array, "dp", split_axis=0, concat_axis=1, tiled=True)

    def from_units(array):
        wide = array.shape[-1]
        array = lax.all_to_all(array, "dp", split_axis=1, concat_axis=0, tiled=True)
        array = array[:unit_count].reshape(heads, micros, tok_rows, wide)
        return array.transpose(1, 2, 0, 3).reshape(tokens, heads, wide)

    projected = (mul(first_low, w_qkv, NN) + qkv_bias.reshape(qkv_wide)).reshape(
        tokens, heads, 3 * HEAD
    )
    grad_att = mul(grad_low, w_out, NN).astype(jnp.bfloat16).reshape(tokens, heads, HEAD)
    packed = to_units(
        jnp.concatenate(
            [
                rotary(projected[..., :HEAD], cosine_table, sine_table).astype(jnp.bfloat16),
                rotary(projected[..., HEAD : 2 * HEAD], cosine_table, sine_table).astype(
                    jnp.bfloat16
                ),
                projected[..., 2 * HEAD :].astype(jnp.bfloat16),
                grad_att,
            ],
            axis=-1,
        )
    )
    unit_ids = lax.axis_index("dp") * units + jnp.arange(units, dtype=jnp.int32)
    unit_out, unit_grads = attention(packed, doc_lengths[unit_ids % micros])
    attended = from_units(unit_out).reshape(tokens, att_wide)
    grad_parts = from_units(unit_grads)

    up_proj = mul(second_low, w_up, NN) + fc1_bias
    activated, gelu_pull = jax.vjp(partial(jax.nn.gelu, approximate=False), up_proj)
    act_low = activated.astype(jnp.bfloat16)
    grad_up = gelu_pull(mul(grad_low, w_down, NN))[0].astype(jnp.bfloat16)
    grad_second = mul(grad_up, w_up, NT)
    branches = lax.psum(
        (mul(attended, w_out, NT) + mul(act_low, w_down, NT)).astype(jnp.bfloat16), "tensor"
    )
    layer_out = (hidden + branches.astype(jnp.float32) + out_bias).astype(jnp.bfloat16)

    early = lax.psum_scatter(
        jnp.concatenate(
            [
                mul(second_low, grad_up, TN).astype(jnp.bfloat16),
                mul(grad_low, act_low, TN).astype(jnp.bfloat16),
                mul(grad_low, attended, TN).astype(jnp.bfloat16),
            ],
            axis=1,
        ),
        "dp",
        scatter_dimension=0,
        tiled=True,
    ).astype(jnp.float32)
    grad_proj = jnp.concatenate(
        [
            rotary(grad_parts[..., :HEAD].astype(jnp.float32), cosine_table, -sine_table),
            rotary(
                grad_parts[..., HEAD : 2 * HEAD].astype(jnp.float32), cosine_table, -sine_table
            ),
            grad_parts[..., 2 * HEAD :].astype(jnp.float32),
        ],
        axis=-1,
    ).astype(jnp.bfloat16)
    grad_proj = grad_proj.reshape(tokens, qkv_wide)
    grad_first = mul(grad_proj, w_qkv, NT)
    grad_unit = (grad_first * norm1_gain + grad_second * norm2_gain).astype(jnp.bfloat16)
    grad_unit, branches_done = lax.optimization_barrier((grad_unit, layer_out))
    grad_unit = lax.psum(grad_unit, "tensor").astype(jnp.float32)
    late = lax.psum_scatter(
        mul(first_low, grad_proj, TN).astype(jnp.bfloat16), "dp", scatter_dimension=0, tiled=True
    ).astype(jnp.float32)
    grad_input = grad_low.astype(jnp.float32) + inverse * (
        grad_unit
        - jnp.mean(grad_unit, axis=-1, keepdims=True)
        - unit_norm * jnp.mean(grad_unit * unit_norm, axis=-1, keepdims=True)
    )
    norm_sums = lax.psum(
        jnp.stack(
            [
                jnp.sum(grad_first * unit_norm, axis=0),
                jnp.sum(grad_first, axis=0),
                jnp.sum(grad_second * unit_norm, axis=0),
                jnp.sum(grad_second, axis=0),
            ]
        ),
        ("dp", "tensor"),
    )
    grad_b_qkv, grad_b_up, grad_b_out = lax.psum(
        (
            jnp.sum(grad_proj.astype(jnp.float32), axis=0),
            jnp.sum(grad_up.astype(jnp.float32), axis=0),
            jnp.sum(grad_low.astype(jnp.float32), axis=0),
        ),
        "dp",
    )
    return (
        branches_done.reshape(hidden_in.shape),
        grad_input.astype(jnp.bfloat16).reshape(hidden_in.shape),
        norm_sums[0],
        norm_sums[1],
        norm_sums[2],
        norm_sums[3],
        late.reshape(shard_rows, heads, 3 * HEAD),
        grad_b_qkv.reshape(heads, 3 * HEAD),
        early[:, 2 * hidden_units :].T.reshape(heads, HEAD, shard_rows),
        grad_b_out,
        early[:, :hidden_units],
        grad_b_up,
        early[:, hidden_units : 2 * hidden_units].T,
    )


def solution(mesh):
    return jax.shard_map(
        shards,
        mesh=mesh,
        in_specs=(
            P(None, "dp", None),
            P(None, "dp", None),
            P(),
            P(),
            P(),
            P(),
            P(),
            P("dp", "tensor", None),
            P("tensor", None),
            P("tensor", None, "dp"),
            P(),
            P("dp", "tensor"),
            P("tensor"),
            P("tensor", "dp"),
        ),
        out_specs=(
            P(None, "dp", None),
            P(None, "dp", None),
            P(),
            P(),
            P(),
            P(),
            P("dp", "tensor", None),
            P("tensor", None),
            P("tensor", None, "dp"),
            P(),
            P("dp", "tensor"),
            P("tensor"),
            P("tensor", "dp"),
        ),
        check_vma=False,
    )
```

time: 1730 us -> 869 us (0.50)
  matrix products: 619 us -> 98.8 us
  waiting for transfers between devices: 724 us -> 368 us
  other arithmetic: 181 us -> 54 us
  Pallas kernels: 0 us -> 72 us
  starting transfers between devices: 1.76 us -> 50.3 us
  local copies, waits for them, and re-layouts: 87.6 us -> 121 us
  loops' own time: 23.3 us -> 0 us
    dot_general x208 -> x12, matrix products: 597 us -> 98.8 us  [mul(): return lax.dot_general(a, b, dims, preferred_element_type=jnp.float32)]
    psum x2, waiting for transfers between devices: 244 us -> 82.8 us  [the longest x1 69.6 us: shards(): lax.psum((mul(attended, w_out, NT) + mul(act_low, w_down, NT)).astype(jnp...]
    reduce_scatter x5 -> x1, waiting for transfers between devices: 155 us -> 9.72 us  [shards(): lax.psum_scatter(mul(first_low, grad_proj, TN).astype(jnp.bfloat16), 'dp'...]
    all_to_all x0 -> x3, waiting for transfers between devices: none -> 137 us  [the longest x1 137 us: to_units(): return lax.all_to_all(array, 'dp', split_axis=0, concat_axis=1, tiled=True)]
    all_gather x7 -> x2, waiting for transfers between devices: 173 us -> 41.4 us  [the longest x1 41.4 us: shards(): lax.all_gather(jnp.concatenate([qkv_weight.reshape(shard_rows, qkv_wide),...]
    reduce_sum x51 -> x5, other arithmetic: 95.4 us -> 19.7 us  [the longest x1 10.5 us: shards(): jnp.sum(grad_first * unit_norm, axis=0)]
    pallas_call x0 -> x2, Pallas kernels: none -> 72 us  [the longest x1 42 us: attention(): pl.pallas_call(partial(attend_back_kernel, rows), grid_spec=pltpu.Prefetc...]
    unnamed x20 -> x7, waiting for transfers between devices: 151 us -> 96.4 us
  transfers between devices with their start and end apart: 17 -> 9, of which waited for: 11 -> 6; matrix products, arithmetic and copies ran while one was open for 38% -> 22% of each run, Pallas kernels for 0% -> 8%
where the time goes in v1:
time: 869 us; the launch traced here: 856 us
  waiting for transfers between devices  368 us (42%)
  local copies, waits for them, and re-layouts  121 us (14%)
  matrix products  98.8 us (11%)
  blocking collectives  77.1 us (9%)
  Pallas kernels  72 us (8%)
  other arithmetic  54 us (6%)
  starting transfers between devices  50.3 us (6%)
  between operations  15.3 us (2%)
    all_to_all x1, waiting for transfers between devices, to_units(): return lax.all_to_all(array, 'dp', split_axis=0, concat_axis=1, tiled=True)  137 us
    dot_general x12, matrix products, mul(): return lax.dot_general(a, b, dims, preferred_element_type=jnp.float32)  98.8 us
    unnamed x7, waiting for transfers between devices  96.4 us
    psum x1, waiting for transfers between devices, shards(): lax.psum((mul(attended, w_out, NT) + mul(act_low, w_down, NT)).astype(jnp...  69.6 us
    all_to_all x2, starting transfers between devices, from_units(): array = lax.all_to_all(array, 'dp', split_axis=1, concat_axis=0, tiled=True)  44.6 us
    pallas_call x1, Pallas kernels, attention(): pl.pallas_call(partial(attend_back_kernel, rows), grid_spec=pltpu.Prefetc...  42 us
    all_gather x1, waiting for transfers between devices, shards(): lax.all_gather(jnp.concatenate([qkv_weight.reshape(shard_rows, qkv_wide),...  41.4 us
    psum x1, blocking collectives, shards(): lax.psum(jnp.stack([jnp.sum(grad_first * unit_norm, axis=0), jnp.sum(grad...  40 us
  transfers between devices with their start and end apart: 9, of which 6 were waited for; matrix products, arithmetic and copies ran while one was open for 22% of the time, Pallas kernels for 8%

profile of v1, /device:TPU:0, one launch (start us, length us, event | category | flops | bytes accessed | tf_op | source)
XLA Modules:
  0.0 856.3 jit_solution(12791686195961059178)
XLA Ops:
  7.3 1.7 pad_maximum_fusion.2
  9.0 2.8 convert_reduce_fusion.1
  11.8 3.0 fusion.15
  16.0 0.9 fusion.54
  17.0 6.1 fusion.26
  23.1 41.4 %all-gather.3.cloned.1.call-done = bf16[1024,1024]{0,1:T(8,128)(2,1)} async-done(((bf16[128,1024]{0,1:T(8,128)(2,1)}), bf16[1024,1024]{0,1:T(8,128)(2,1)}) %all-gather.3.cloned.1.call-update) | async-done | bytes 2097168 | tf_op jit(solution)/shard_map/all_gather | solution.py:214
  64.5 5.7 convolution_add_fusion
  70.7 1.2 fusion.60
  72.8 1.8 copy.112
  74.7 1.7 copy.108
  76.4 1.7 copy.109
  78.1 1.7 copy.111
  79.8 2.7 copy.113
  82.5 2.7 copy.110
  85.2 1.7 copy.114
  86.9 4.6 fusion.38
  91.6 1.8 concatenate.47
  93.4 2.5 copy.115
  95.9 17.2 %concatenate.48 = bf16[4,512,4,256]{3,1,0,2:T(8,128)(2,1)} concatenate(bf16[4,512,4,8]{3,1,0,2:T(8,128)(2,1)} %bitcast.168, bf16[4,512,4,8]{3,1,0,2:T(8,128)(2,1)} %bitcast.169, bf16[4,512,4,48]{3,1,0,2:T(8,128)(2,1)} %bitcast.172, bf16[4,512,4,8]{3,1,0,2:T(8,128)(2,1)} %bitcast.170, bf16[4,512,4,8]{3,1,0,2:T(8,128)(2,1)S(1)} %bitcast.167, bf16[4,512,4,48]{3,1,0,2:T(8,128)(2,1)} %bitcast.171, ...), dimensions={3} | concatenate | bytes 8388608 | tf_op jit(solution)/shard_map/concatenate | solution.py:259
  113.1 4.7 all-to-all-start
  118.3 0.8 pad_maximum_fusion.1
  120.7 137.2 %all-to-all-done = bf16[16,512,256]{2,1,0:T(8,128)(2,1)} async-done(((bf16[16,512,256]{2,1,0:T(8,128)(2,1)}), bf16[16,512,256]{2,1,0:T(8,128)(2,1)}, u32[]{:S(2)}, u32[]{:S(2)}) %all-to-all-start) | async-done | bytes 4194336 | tf_op jit(solution)/shard_map/all_to_all | solution.py:246
  257.9 2.6 copy.116
  260.5 30.1 %shard_map.237 = (bf16[2,4096,64]{2,1,0:T(8,128)(2,1)S(1)}, f32[2,1,4096]{2,1,0:T(1,128)S(1)}, f32[2,1,4096]{2,1,0:T(1,128)S(1)}) custom-call(s32[2,8]{1,0:T(2,128)S(1)} %and_select_fusion.first_ref, bf16[2,4096,256]{2,1,0:T(8,128)(2,1)S(1)} %bitcast.155, s32[2,1,4096]{2,1,0:T(1,128)S(1)} %broadcast_in_dim.27.start_ref), custom_call_target="tpu_custom_call" | custom-call | flops 8589934592 | bytes 5734400 | tf_op jit(solution)/shard_map/pallas_call | solution.py:152
  290.6 17.8 %copy.142 = bf16[2,4096,64]{2,0,1:T(2,128)(2,1)S(1)} copy(bf16[2,4096,64]{2,1,0:T(8,128)(2,1)S(1)} %get-tuple-element.20) | data formatting | bytes 2097152 | tf_op jit(solution)/shard_map/pallas_call | solution.py:152
  308.4 2.7 reshape.351
  311.0 17.1 %all-to-all-start.2 = ((bf16[8,2,32768]{2,1,0:T(2,128)(2,1)}), bf16[8,2,32768]{2,1,0:T(2,128)(2,1)S(1)}, u32[]{:S(2)}, u32[]{:S(2)}) async-start(bf16[8,2,32768]{2,1,0:T(2,128)(2,1)} %reshape.351), calls=%async_computation.2 | async-start | bytes 2097152 | tf_op jit(solution)/shard_map/all_to_all | solution.py:250
  328.2 2.2 copy-done.1
  330.4 42.0 %shard_map.238 = bf16[2,4096,192]{2,1,0:T(8,128)(2,1)S(1)} custom-call(s32[2,8]{1,0:T(2,128)S(1)} %and_select_fusion.1.last_ref, bf16[2,4096,256]{2,1,0:T(8,128)(2,1)S(1)} %bitcast.156, s32[2,1,4096]{2,1,0:T(1,128)S(1)} %broadcast_in_dim.27.start_ref, f32[2,1,4096]{2,1,0:T(1,128)S(1)} %get-tuple-element.18.lse_ref, f32[2,1,4096]{2,1,0:T(1,128)S(1)} %get-tuple-element.19.delta_ref), custom_call_target="tpu_custom_call" | custom-call | flops 21474836480 | bytes 8192000 | tf_op jit(solution)/shard_map/pallas_call | solution.py:170
  372.3 27.2 %copy.117 = bf16[2,4096,192]{2,0,1:T(2,128)(2,1)} copy(bf16[2,4096,192]{2,1,0:T(8,128)(2,1)S(1)} %shard_map.238) | data formatting | bytes 6291456 | tf_op jit(solution)/shard_map/pallas_call | solution.py:170
  399.5 27.4 %all-to-all-start.1 = ((bf16[2,4096,192]{2,0,1:T(2,128)(2,1)}), bf16[2,4096,192]{2,0,1:T(2,128)(2,1)}, u32[]{:S(2)}, u32[]{:S(2)}) async-start(bf16[2,4096,192]{2,0,1:T(2,128)(2,1)} %copy.117), calls=%async_computation.1 | async-start | bytes 8388608 | tf_op jit(solution)/shard_map/all_to_all | solution.py:250
  427.4 26.3 %multiply_convert_fusion = (bf16[2048,1024]{1,0:T(8,128)(2,1)S(1)}, f32[2048,1024]{1,0:T(8,128)}, f32[2048,1024]{1,0:T(8,128)}) fusion(f32[1024]{0:T(1024)S(1)} %copy-done.31, bf16[2048,1024]{1,0:T(8,128)(2,1)} %get-tuple-element.121, bf16[1024,2048]{0,1:T(8,128)(2,1)} %all-gather.5.cloned.1.call-done), kind=kOutput, calls=%fused_computation.47 | convolution fusion | flops 4433379328 | bytes 27267072 | tf_op jit(solution)/shard_map/dot_general | solution.py:56
  453.8 1.9 copy-done.33
  455.7 6.8 fusion.39
  462.5 1.4 reshape.352
  464.0 1.4 copy.133
  465.4 0.8 copy.126
  466.5 1.0 copy-done.4
  467.5 6.9 add_convert_fusion
  474.7 17.4 %convert_reduce_fusion.2 = (f32[1024]{0:T(1024)S(1)}, bf16[2048,1024]{1,0:T(8,128)(2,1)}) fusion(f32[2048,1024]{1,0:T(8,128)} %get-tuple-element.115, bf16[2048,1024]{1,0:T(8,128)(2,1)} %bitcast.159, bf16[1024,2048]{0,1:T(8,128)(2,1)} %all-gather.5.cloned.1.call-done, f32[2048,1024]{1,0:T(8,128)} %get-tuple-element.137, f32[1024]{0:T(1024)S(1)} %copy-done.31), kind=kOutput, calls=%fused_computation.44 | convolution fusion | flops 4330617856 | bytes 27271168 | tf_op jit(solution)/shard_map/dot_general | solution.py:56
  492.1 69.6 %all-reduce.4.cloned.1.call-done = bf16[2048,1024]{1,0:T(8,128)(2,1)} async-done(((bf16[2048,1024]{1,0:T(8,128)(2,1)}), bf16[2048,1024]{1,0:T(8,128)(2,1)}) %all-reduce.4.cloned.1.call-update) | async-done | bytes 4194320 | tf_op jit(solution)/shard_map/psum | solution.py:281
  561.6 7.6 fusion.32
  569.3 9.3 %copy.131 = bf16[2,8,512,192]{2,3,0,1:T(8,128)(2,1)S(1)} copy(bf16[2,8,512,192]{3,0,2,1:T(2,128)(2,1)} %bitcast.20) | data formatting | bytes 6291456 | tf_op jit(solution)/shard_map/all_to_all | solution.py:250
  580.6 3.5 fusion.46
  584.2 8.3 add_convert_fusion.1
  592.7 3.3 fusion.18
  596.0 4.8 convolution_convert_fusion.2
  600.8 8.2 convolution_convert_fusion.1
  609.0 5.0 convert_bitcast_fusion
  614.1 1.3 fusion.49
  615.4 2.6 pad_maximum_fusion
  617.9 6.7 copy.134
  624.7 2.9 convert_reduce_fusion.3
  628.0 37.1 %all-reduce = (f32[4,192]{1,0:T(4,128)}, f32[1024]{0:T(1024)}, f32[1024]{0:T(1024)}) all-reduce(f32[4,192]{1,0:T(4,128)S(1)} %convert_reduce_fusion.4, f32[1024]{0:T(1024)S(1)} %convert_reduce_fusion.3, f32[1024]{0:T(1024)S(1)} %get-tuple-element.140), channel_id=1, replica_groups=mesh['dp'=8,'tensor'=4] {'dp'}, use_global_device_ids=true, to_apply=%region_18.19 | all-reduce | flops 2816 | bytes 22528 | tf_op jit(solution)/shard_map/psum | solution.py:333
  665.1 13.3 %all-reduce.6.cloned.1.call-done = bf16[2048,1024]{1,0:T(8,128)(2,1)} async-done(((bf16[2048,1024]{1,0:T(8,128)(2,1)}), bf16[2048,1024]{1,0:T(8,128)(2,1)}) %all-reduce.6.cloned.1.call-update) | async-done | bytes 4194320 | tf_op jit(solution)/shard_map/psum | solution.py:313
  678.4 10.5 %fusion.29 = (f32[1024]{0:T(1024)S(1)}, f32[1024]{0:T(1024)S(1)}, f32[2048]{0:T(1024)S(1)}, f32[1024]{0:T(1024)S(1)}, f32[1024]{0:T(1024)S(1)}, /*index=5*/f32[2048]{0:T(1024)S(1)}) fusion(f32[2048,1024]{1,0:T(8,128)} %copy-done.3, bf16[4,512,1024]{2,1,0:T(8,128)(2,1)} %param.14, f32[2048]{0:T(1024)S(1)} %bitcast.189, f32[2048]{0:T(1024)S(1)} %bitcast.192, ...), kind=kLoop, calls=%fused_computation.40 | loop fusion | flops 27254784 | bytes 25214976 | tf_op jit(solution)/shard_map/reduce_sum | solution.py:325
  689.0 40.0 %psum.44 = f32[4,1024]{1,0:T(4,128)S(1)} all-reduce(f32[4,1024]{1,0:T(4,128)S(1)} %pad_maximum_fusion.3), channel_id=1, replica_groups=mesh['dp'=8,'tensor'=4] {'dp','tensor'}, use_global_device_ids=true, to_apply=%region_15.16 | all-reduce | flops 4096 | bytes 32768 | tf_op jit(solution)/shard_map/psum | solution.py:322
  729.5 7.6 fusion.4
  737.2 9.7 %reduce-scatter.5.cloned.1.call-done = bf16[128,768]{1,0:T(8,128)(2,1)} async-done(((bf16[1024,768]{1,0:T(8,128)(2,1)}), bf16[128,768]{1,0:T(8,128)(2,1)}) %reduce-scatter.5.cloned.1.call-update) | async-done | bytes 196624 | tf_op jit(solution)/shard_map/reduce_scatter | solution.py:314
  746.9 1.8 copy.127
  748.7 96.3 %reduce-scatter.7.cloned.1.call-done = bf16[128,2304]{1,0:T(8,128)(2,1)} async-done(((bf16[1024,2304]{1,0:T(8,128)(2,1)}), bf16[128,2304]{1,0:T(8,128)(2,1)}) %reduce-scatter.7.cloned.1.call-update) | async-done | bytes 589840
  845.1 1.4 copy.135
  847.2 0.8 slice_bitcast_fusion
  848.1 1.0 copy.128
  (126 shorter events, 9.5 us)
Async XLA Ops:
  7.2 8.3 copy-start.28
  7.2 8.4 copy-start.18
  7.2 9.7 %copy-start.22 = (f32[1024]{0:T(1024)S(1)}, f32[1024]{0:T(1024)}, u32[]{:S(2)}) copy-start(f32[1024]{0:T(1024)} %param.17) | copy-start | bytes 12292
  7.2 9.7 %copy-start.20 = (f32[1024]{0:T(1024)S(1)}, f32[1024]{0:T(1024)}, u32[]{:S(2)}) copy-start(f32[1024]{0:T(1024)} %param.18) | copy-start | bytes 12292
  7.2 9.7 %copy-start.26 = (f32[1024]{0:T(1024)S(1)}, f32[1024]{0:T(1024)}, u32[]{:S(2)}) copy-start(f32[1024]{0:T(1024)} %param.19) | copy-start | bytes 12292
  7.2 9.7 %copy-start.24 = (f32[1024]{0:T(1024)S(1)}, f32[1024]{0:T(1024)}, u32[]{:S(2)}) copy-start(f32[1024]{0:T(1024)} %param.20) | copy-start | bytes 12292
  7.2 57.3 %all-gather.3.cloned.1.call-start = ((), (), s32[]{:S(2)}) async-start(), calls=%async_computation.5 | async-start | bytes 2359296 | tf_op jit(solution)/shard_map/all_gather | solution.py:214
  11.8 3.6 copy-start.16
  15.5 54.8 %copy-start.11 = (f32[1,4,4,128]{3,1,2,0:T(4,128)}, f32[1,4,4,128]{3,1,2,0:T(4,128)S(1)}, u32[]{:S(2)}) copy-start(f32[1,4,4,128]{3,1,2,0:T(4,128)S(1)} %copy.138) | copy-start | bytes 24580
  15.5 54.8 %copy-start.13 = (f32[1,4,4,128]{3,1,2,0:T(4,128)}, f32[1,4,4,128]{3,1,2,0:T(4,128)S(1)}, u32[]{:S(2)}) copy-start(f32[1,4,4,128]{3,1,2,0:T(4,128)S(1)} %copy.137) | copy-start | bytes 24580
  16.9 55.1 %copy-start.6 = (f32[2048,8]{0,1:T(8,128)}, f32[2048,8]{0,1:T(8,128)S(1)}, u32[]{:S(2)}) copy-start(f32[2048,8]{0,1:T(8,128)S(1)} %get-tuple-element.132) | copy-start | bytes 196612
  113.1 5.0 copy-start.9
  113.1 5.2 copy-start.10
  113.1 144.8 %all-to-all-start = ((bf16[16,512,256]{2,1,0:T(8,128)(2,1)}), bf16[16,512,256]{2,1,0:T(8,128)(2,1)}, u32[]{:S(2)}, u32[]{:S(2)}) async-start(bf16[16,512,256]{2,1,0:T(8,128)(2,1)} %bitcast.157), calls=%async_computation | async-start | bytes 8388608 | tf_op jit(solution)/shard_map/all_to_all | solution.py:246
  117.8 309.6 %all-gather.5.cloned.1.call-start = ((), (), s32[]{:S(2)}) async-start(), calls=%async_computation.6 | async-start | bytes 4718592 | tf_op jit(solution)/shard_map/all_gather | solution.py:224
  260.5 30.1 %copy-start = (bf16[2,8,512,256]{3,2,1,0:T(8,128)(2,1)}, bf16[2,8,512,256]{3,2,1,0:T(8,128)(2,1)S(1)}, u32[]{:S(2)}) copy-start(bf16[2,8,512,256]{3,2,1,0:T(8,128)(2,1)S(1)} %copy.116) | copy-start | bytes 12582916
  311.0 88.5 %all-to-all-start.2 = ((bf16[8,2,32768]{2,1,0:T(2,128)(2,1)}), bf16[8,2,32768]{2,1,0:T(2,128)(2,1)S(1)}, u32[]{:S(2)}, u32[]{:S(2)}) async-start(bf16[8,2,32768]{2,1,0:T(2,128)(2,1)} %reshape.351), calls=%async_computation.2 | async-start | bytes 2097152 | tf_op jit(solution)/shard_map/all_to_all | solution.py:250
  328.2 2.2 copy-start.1
  372.3 55.1 %copy-start.31 = (f32[1024]{0:T(1024)S(1)}, f32[1024]{0:T(1024)}, u32[]{:S(2)}) copy-start(f32[1024]{0:T(1024)} %param.26) | copy-start | bytes 12292
  399.5 169.7 %all-to-all-start.1 = ((bf16[2,4096,192]{2,0,1:T(2,128)(2,1)}), bf16[2,4096,192]{2,0,1:T(2,128)(2,1)}, u32[]{:S(2)}, u32[]{:S(2)}) async-start(bf16[2,4096,192]{2,0,1:T(2,128)(2,1)} %copy.117), calls=%async_computation.1 | async-start | bytes 8388608 | tf_op jit(solution)/shard_map/all_to_all | solution.py:250
  427.0 134.7 %all-reduce.4.cloned.1.call-start = ((), (), s32[]{:S(2)}) async-start(), calls=%async_computation.7 | async-start | bytes 8388608 | tf_op jit(solution)/shard_map/psum | solution.py:281
  427.4 28.3 %copy-start.29 = (bf16[1024,2048]{0,1:T(8,128)(2,1)S(1)}, bf16[1024,2048]{0,1:T(8,128)(2,1)}, u32[]{:S(2)}) copy-start(bf16[1024,2048]{0,1:T(8,128)(2,1)} %all-gather.5.cloned.1.call-done) | copy-start | bytes 12582916
  453.8 1.9 copy-start.33
  466.5 1.0 copy-start.4
  474.5 203.9 %all-reduce.6.cloned.1.call-start = ((), (), s32[]{:S(2)}) async-start(), calls=%async_computation.8 | async-start | bytes 8388608 | tf_op jit(solution)/shard_map/psum | solution.py:313
  474.7 87.0 %copy-start.25 = (f32[1024]{0:T(1024)S(1)}, f32[1024]{0:T(1024)}, u32[]{:S(2)}) copy-start(f32[1024]{0:T(1024)} %param.24) | copy-start | bytes 12292
  569.3 10.3 %copy-start.7 = (f32[2048,8]{0,1:T(8,128)S(1)}, f32[2048,8]{0,1:T(8,128)}, u32[]{:S(2)}) copy-start(f32[2048,8]{0,1:T(8,128)} %copy-done.6) | copy-start | bytes 196612
  569.3 10.3 %copy-start.8 = (f32[2048,8]{0,1:T(8,128)S(1)}, f32[2048,8]{0,1:T(8,128)}, u32[]{:S(2)}) copy-start(f32[2048,8]{0,1:T(8,128)} %get-tuple-element.130) | copy-start | bytes 196612
  579.0 1.6 copy-start.15
  580.6 3.5 copy-start.23
  580.6 3.5 copy-start.27
  580.6 3.5 copy-start.30
  580.6 3.6 copy-start.32
  584.1 8.4 copy-start.3
  584.2 8.4 copy-start.17
  584.2 8.4 copy-start.19
  584.2 8.4 copy-start.21
  592.6 154.3 %reduce-scatter.5.cloned.1.call-start = ((), (), s32[]{:S(2)}) async-start(), calls=%async_computation.9 | async-start | bytes 1769472 | tf_op jit(solution)/shard_map/reduce_scatter | solution.py:314
  600.7 244.3 %reduce-scatter.7.cloned.1.call-start = ((), (), s32[]{:S(2)}) async-start(), calls=%async_computation.10 | async-start | bytes 5308416
  600.8 8.2 copy-start.2
  600.8 8.2 copy-start.34
  609.0 5.0 copy-start.5
  624.6 53.7 %copy-start.12 = (f32[1,4,4,128]{3,1,2,0:T(4,128)S(1)}, f32[1,4,4,128]{3,1,2,0:T(4,128)}, u32[]{:S(2)}) copy-start(f32[1,4,4,128]{3,1,2,0:T(4,128)} %copy-done.11) | copy-start | bytes 24580
  624.6 53.7 %copy-start.14 = (f32[1,4,4,128]{3,1,2,0:T(4,128)S(1)}, f32[1,4,4,128]{3,1,2,0:T(4,128)}, u32[]{:S(2)}) copy-start(f32[1,4,4,128]{3,1,2,0:T(4,128)} %copy-done.13) | copy-start | bytes 24580
Sparse Core Ops, SparseCore 0:
  10.7 53.7 all-gather.2
  121.3 140.2 all-gather.4
  474.6 87.0 all-reduce.3
  592.7 85.6 all-reduce.5
  681.6 65.2 reduce-scatter.4
  750.9 94.1 reduce-scatter.6

commit v2 on v1

v2 whole, which is shorter than its diff:
```python
from functools import partial
import math

import jax
import jax.numpy as jnp
from jax import lax
from jax.experimental import pallas as pl
from jax.experimental.pallas import tpu as pltpu
from jax.sharding import PartitionSpec as P

HEAD = 64
ROT = 16


norm_epsilon = 1e-05
masked_score = -1e30


def documents(lengths, token_index):
    bounds = jnp.cumsum(lengths)
    passed = bounds[None, :] <= token_index[:, None]
    segment = jnp.sum(passed.astype(jnp.int32), axis=1)
    doc_start = jnp.max(jnp.where(passed, bounds[None, :], 0), axis=1)
    return (segment, token_index - doc_start)


def rotary_angles(position):
    half_width = ROT // 2
    frequency = jnp.power(10000.0, -2.0 * jnp.arange(half_width, dtype=jnp.float32) / ROT)
    angles = position.astype(jnp.float32)[..., None] * frequency
    return (jnp.cos(angles)[..., None, :], jnp.sin(angles)[..., None, :])


def rotary(vectors, cosine_table, sine_table):
    half_width = cosine_table.shape[-1]
    lower_half = vectors[..., :half_width]
    upper_half = vectors[..., half_width : 2 * half_width]
    return jnp.concatenate(
        [
            lower_half * cosine_table - upper_half * sine_table,
            upper_half * cosine_table + lower_half * sine_table,
            vectors[..., 2 * half_width :],
        ],
        axis=-1,
    )


NT = (((1,), (1,)), ((), ()))
TN = (((0,), (0,)), ((), ()))
NN = (((1,), (0,)), ((), ()))
score_scale = HEAD**-0.5
vmem_bytes = 44 * 1024 * 1024


def mul(a, b, dims):
    return lax.dot_general(a, b, dims, preferred_element_type=jnp.float32)


def attend_kernel(units, first_ref, x_ref, start_ref, out_ref, lse_ref, delta_ref):
    block = pl.program_id(0)
    rows = x_ref.shape[1]
    query_index = block * rows + lax.broadcasted_iota(jnp.int32, (1, rows), 1)
    for unit in range(units):
        base = unit * 4 * HEAD
        own = x_ref[block, :, base : base + 4 * HEAD]
        queries = own[:, :HEAD] * jnp.bfloat16(score_scale)
        grad_att = own[:, 3 * HEAD :]
        start = start_ref[unit]

        def step(key_block, carry):
            top, total, acc = carry
            piece = x_ref[key_block, :, base : base + 4 * HEAD]
            scores = mul(piece[:, HEAD : 2 * HEAD], queries, NT)
            key_index = key_block * rows + lax.broadcasted_iota(jnp.int32, (rows, rows), 0)
            allowed = (key_index <= query_index) & (key_index >= start)
            scores = jnp.where(allowed, scores, masked_score)
            new_top = jnp.maximum(top, jnp.max(scores, axis=0, keepdims=True))
            decay = jnp.exp(top - new_top)
            exponent = jnp.exp(scores - new_top)
            total = total * decay + jnp.sum(exponent, axis=0, keepdims=True)
            acc = acc * decay + mul(
                piece[:, 2 * HEAD : 3 * HEAD], exponent.astype(jnp.bfloat16), TN
            )
            return (new_top, total, acc)

        top, total, acc = lax.fori_loop(
            first_ref[unit, block],
            block + 1,
            step,
            (
                jnp.full((1, rows), masked_score, jnp.float32),
                jnp.zeros((1, rows), jnp.float32),
                jnp.zeros((HEAD, rows), jnp.float32),
            ),
        )
        attended = acc / total
        lse_ref[unit] = top + jnp.log(total)
        delta_ref[unit] = jnp.sum(attended * grad_att.astype(jnp.float32).T, axis=0, keepdims=True)
        out_ref[0, :, unit * HEAD : (unit + 1) * HEAD] = attended.T.astype(jnp.bfloat16)


def attend_back_kernel(units, last_ref, x_ref, start_ref, lse_ref, delta_ref, grad_ref, grad_q):
    block = pl.program_id(0)
    rows = x_ref.shape[1]
    key_index = block * rows + lax.broadcasted_iota(jnp.int32, (rows, rows), 0)

    @pl.when(block == 0)
    def _():
        grad_q[...] = jnp.zeros_like(grad_q)

    for unit in range(units):
        base = unit * 4 * HEAD
        own = x_ref[block, :, base : base + 4 * HEAD]
        keys, values = own[:, HEAD : 2 * HEAD], own[:, 2 * HEAD : 3 * HEAD]

        def step(query_block, carry):
            grad_keys, grad_values = carry
            there = pl.ds(pl.multiple_of(query_block * rows, rows), rows)
            piece = x_ref[query_block, :, base : base + 4 * HEAD]
            queries = piece[:, :HEAD] * jnp.bfloat16(score_scale)
            grad_att = piece[:, 3 * HEAD :]
            query_index = query_block * rows + lax.broadcasted_iota(jnp.int32, (1, rows), 1)
            allowed = (key_index <= query_index) & (key_index >= start_ref[unit, :, there])
            scores = mul(keys, queries, NT)
            probs = jnp.where(allowed, jnp.exp(scores - lse_ref[unit, :, there]), 0.0)
            grad_values = grad_values + mul(probs.astype(jnp.bfloat16), grad_att, NN)
            grad_probs = mul(values, grad_att, NT)
            grad_scores = (probs * (grad_probs - delta_ref[unit, :, there])).astype(jnp.bfloat16)
            grad_keys = grad_keys + mul(grad_scores, queries, NN)
            grad_q[unit, query_block] += mul(grad_scores, keys, TN)
            return (grad_keys, grad_values)

        zero = jnp.zeros((rows, HEAD), jnp.float32)
        grad_keys, grad_values = lax.fori_loop(
            block, last_ref[unit, block] + 1, step, (zero, zero)
        )
        base = unit * 3 * HEAD
        grad_ref[0, :, base : base + HEAD] = (grad_q[unit, block] * score_scale).astype(
            jnp.bfloat16
        )
        grad_ref[0, :, base + HEAD : base + 2 * HEAD] = grad_keys.astype(jnp.bfloat16)
        grad_ref[0, :, base + 2 * HEAD : base + 3 * HEAD] = grad_values.astype(jnp.bfloat16)


def attention(packed, lengths):
    blocks, rows, width = packed.shape
    units = width // (4 * HEAD)
    length = blocks * rows
    bounds = jnp.cumsum(lengths, axis=1)[:, None, :]
    token = jnp.arange(length, dtype=jnp.int32)[None, :, None]
    start = jnp.max(jnp.where(bounds <= token, bounds, 0), axis=2)
    end = jnp.min(jnp.where(bounds > token, bounds, length), axis=2)
    first = start[:, ::rows] // rows
    last = (end[:, rows - 1 :: rows] - 1) // rows
    start = start[:, None, :]
    whole = pl.BlockSpec((blocks, rows, width), lambda b, s: (0, 0, 0))
    line = pl.BlockSpec((units, 1, rows), lambda b, s: (0, 0, b))
    full_line = pl.BlockSpec((units, 1, length), lambda b, s: (0, 0, 0))
    pairs = units * length * length // 4
    out, lse, delta = pl.pallas_call(
        partial(attend_kernel, units),
        grid_spec=pltpu.PrefetchScalarGridSpec(
            num_scalar_prefetch=1,
            grid=(blocks,),
            in_specs=[whole, line],
            out_specs=[
                pl.BlockSpec((1, rows, units * HEAD), lambda b, s: (b, 0, 0)),
                line,
                line,
            ],
        ),
        out_shape=[
            jax.ShapeDtypeStruct((blocks, rows, units * HEAD), jnp.bfloat16),
            jax.ShapeDtypeStruct((units, 1, length), jnp.float32),
            jax.ShapeDtypeStruct((units, 1, length), jnp.float32),
        ],
        compiler_params=pltpu.CompilerParams(vmem_limit_bytes=vmem_bytes),
        cost_estimate=pl.CostEstimate(
            flops=pairs * 4 * 256, bytes_accessed=units * length * 700, transcendentals=pairs
        ),
    )(first, packed, start)
    grads = pl.pallas_call(
        partial(attend_back_kernel, units),
        grid_spec=pltpu.PrefetchScalarGridSpec(
            num_scalar_prefetch=1,
            grid=(blocks,),
            in_specs=[whole, full_line, full_line, full_line],
            out_specs=pl.BlockSpec((1, rows, units * 3 * HEAD), lambda b, s: (b, 0, 0)),
            scratch_shapes=[pltpu.VMEM((units, blocks, rows, HEAD), jnp.float32)],
        ),
        out_shape=jax.ShapeDtypeStruct((blocks, rows, units * 3 * HEAD), jnp.bfloat16),
        compiler_params=pltpu.CompilerParams(vmem_limit_bytes=vmem_bytes),
        cost_estimate=pl.CostEstimate(
            flops=pairs * 10 * 256, bytes_accessed=units * length * 1000, transcendentals=pairs
        ),
    )(last, packed, start, lse, delta)
    return (out, grads)


def shards(
    hidden_in,
    cotangent,
    doc_lengths,
    norm1_gain,
    norm1_bias,
    norm2_gain,
    norm2_bias,
    qkv_weight,
    qkv_bias,
    out_weight,
    out_bias,
    fc1_weight,
    fc1_bias,
    fc2_weight,
):
    micros, tok_rows, width = hidden_in.shape
    heads = qkv_bias.shape[0]
    hidden_units = fc1_bias.shape[0]
    shard_rows = qkv_weight.shape[0]
    dp_count = lax.axis_size("dp")
    tokens = micros * tok_rows
    qkv_wide, att_wide = heads * 3 * HEAD, heads * HEAD
    unit_count = micros * heads
    units = -(-unit_count // dp_count)

    att_weights = lax.all_gather(
        jnp.concatenate(
            [qkv_weight.reshape(shard_rows, qkv_wide), out_weight.reshape(att_wide, shard_rows).T],
            axis=1,
        ),
        "dp",
        axis=0,
        tiled=True,
    )
    w_qkv, w_out = att_weights[:, :qkv_wide], att_weights[:, qkv_wide:]
    ff_weights = lax.all_gather(
        jnp.concatenate([fc1_weight, fc2_weight.T], axis=1), "dp", axis=0, tiled=True
    )
    w_up, w_down = ff_weights[:, :hidden_units], ff_weights[:, hidden_units:]

    query_index = lax.axis_index("dp") * tok_rows + jnp.arange(tok_rows, dtype=jnp.int32)
    position = jax.vmap(lambda lengths: documents(lengths, query_index)[1])(doc_lengths)
    cosine_table, sine_table = rotary_angles(position.reshape(tokens))
    hidden = hidden_in.reshape(tokens, width).astype(jnp.float32)
    grad_low = cotangent.reshape(tokens, width)
    centered = hidden - jnp.mean(hidden, axis=-1, keepdims=True)
    variance = jnp.mean(centered * centered, axis=-1, keepdims=True)
    inverse = lax.rsqrt(variance + norm_epsilon)
    unit_norm = centered * inverse
    first_low = (unit_norm * norm1_gain + norm1_bias).astype(jnp.bfloat16)
    second_low = (unit_norm * norm2_gain + norm2_bias).astype(jnp.bfloat16)

    def to_units(array):
        wide = array.shape[-1]
        array = array.reshape(micros, tok_rows, heads, wide).transpose(2, 0, 1, 3)
        array = array.reshape(unit_count, tok_rows, wide)
        if units * dp_count > unit_count:
            array = jnp.pad(array, ((0, units * dp_count - unit_count), (0, 0), (0, 0)))
        array = array.reshape(dp_count, units, tok_rows, wide).transpose(0, 2, 1, 3)
        array = array.reshape(dp_count, tok_rows, units * wide)
        return lax.all_to_all(array, "dp", split_axis=0, concat_axis=0, tiled=True)

    def from_units(array):
        wide = array.shape[-1] // units
        array = lax.all_to_all(array, "dp", split_axis=0, concat_axis=0, tiled=True)
        array = array.reshape(dp_count, tok_rows, units, wide).transpose(0, 2, 1, 3)
        array = array.reshape(units * dp_count, tok_rows, wide)
        array = array[:unit_count].reshape(heads, micros, tok_rows, wide)
        return array.transpose(1, 2, 0, 3).reshape(tokens, heads, wide)

    projected = (mul(first_low, w_qkv, NN) + qkv_bias.reshape(qkv_wide)).reshape(
        tokens, heads, 3 * HEAD
    )
    grad_att = mul(grad_low, w_out, NN).astype(jnp.bfloat16).reshape(tokens, heads, HEAD)
    packed = to_units(
        jnp.concatenate(
            [
                rotary(projected[..., :HEAD], cosine_table, sine_table).astype(jnp.bfloat16),
                rotary(projected[..., HEAD : 2 * HEAD], cosine_table, sine_table).astype(
                    jnp.bfloat16
                ),
                projected[..., 2 * HEAD :].astype(jnp.bfloat16),
                grad_att,
            ],
            axis=-1,
        )
    )
    up_proj = mul(second_low, w_up, NN) + fc1_bias
    activated, gelu_pull = jax.vjp(partial(jax.nn.gelu, approximate=False), up_proj)
    act_low = activated.astype(jnp.bfloat16)
    grad_up = gelu_pull(mul(grad_low, w_down, NN))[0].astype(jnp.bfloat16)
    grad_second = mul(grad_up, w_up, NT)
    ff_grads = jnp.concatenate(
        [
            mul(second_low, grad_up, TN).astype(jnp.bfloat16),
            mul(grad_low, act_low, TN).astype(jnp.bfloat16),
        ],
        axis=1,
    )
    down = mul(act_low, w_down, NT)
    packed, ff_grads, down, grad_second = lax.optimization_barrier(
        (packed, ff_grads, down, grad_second)
    )
    early = lax.psum_scatter(ff_grads, "dp", scatter_dimension=0, tiled=True).astype(jnp.float32)
    unit_ids = lax.axis_index("dp") * units + jnp.arange(units, dtype=jnp.int32)
    unit_out, unit_grads = attention(packed, doc_lengths[unit_ids % micros])
    attended = from_units(unit_out).reshape(tokens, att_wide)
    grad_parts = from_units(unit_grads)

    branches = lax.psum(
        (mul(attended, w_out, NT) + down).astype(jnp.bfloat16), "tensor"
    )
    layer_out = (hidden + branches.astype(jnp.float32) + out_bias).astype(jnp.bfloat16)

    grad_proj = jnp.concatenate(
        [
            rotary(grad_parts[..., :HEAD].astype(jnp.float32), cosine_table, -sine_table),
            rotary(
                grad_parts[..., HEAD : 2 * HEAD].astype(jnp.float32), cosine_table, -sine_table
            ),
            grad_parts[..., 2 * HEAD :].astype(jnp.float32),
        ],
        axis=-1,
    ).astype(jnp.bfloat16)
    grad_proj = grad_proj.reshape(tokens, qkv_wide)
    grad_first = mul(grad_proj, w_qkv, NT)
    grad_unit = (grad_first * norm1_gain + grad_second * norm2_gain).astype(jnp.bfloat16)
    grad_unit, branches_done = lax.optimization_barrier((grad_unit, layer_out))
    grad_unit = lax.psum(grad_unit, "tensor").astype(jnp.float32)
    late = lax.psum_scatter(
        jnp.concatenate(
            [
                mul(first_low, grad_proj, TN).astype(jnp.bfloat16),
                mul(grad_low, attended, TN).astype(jnp.bfloat16),
            ],
            axis=1,
        ),
        "dp", scatter_dimension=0, tiled=True
    ).astype(jnp.float32)
    grad_input = grad_low.astype(jnp.float32) + inverse * (
        grad_unit
        - jnp.mean(grad_unit, axis=-1, keepdims=True)
        - unit_norm * jnp.mean(grad_unit * unit_norm, axis=-1, keepdims=True)
    )
    mine = lax.axis_index("tensor")
    split = jnp.concatenate(
        [
            jnp.sum(grad_proj.astype(jnp.float32), axis=0),
            jnp.sum(grad_up.astype(jnp.float32), axis=0),
        ]
    )
    slots = jnp.arange(lax.axis_size("tensor"), dtype=jnp.int32)[:, None] == mine
    slots = jnp.where(slots, split[None, :], 0.0)
    sums = jnp.concatenate(
        [
            jnp.sum(grad_first * unit_norm, axis=0),
            jnp.sum(grad_first, axis=0),
            jnp.sum(grad_second * unit_norm, axis=0),
            jnp.sum(grad_second, axis=0),
            jnp.where(mine == 0, jnp.sum(grad_low.astype(jnp.float32), axis=0), 0.0),
            slots.reshape(-1),
        ]
    )
    sums = lax.psum(sums.reshape(-1, 128), ("dp", "tensor")).reshape(-1)
    norm_sums = sums[: 4 * width].reshape(4, width)
    grad_b_out = sums[4 * width : 5 * width]
    split = lax.dynamic_index_in_dim(sums[5 * width :].reshape(slots.shape), mine, 0, False)
    grad_b_qkv, grad_b_up = split[:qkv_wide], split[qkv_wide:]
    return (
        branches_done.reshape(hidden_in.shape),
        grad_input.astype(jnp.bfloat16).reshape(hidden_in.shape),
        norm_sums[0],
        norm_sums[1],
        norm_sums[2],
        norm_sums[3],
        late[:, :qkv_wide].reshape(shard_rows, heads, 3 * HEAD),
        grad_b_qkv.reshape(heads, 3 * HEAD),
        late[:, qkv_wide:].T.reshape(heads, HEAD, shard_rows),
        grad_b_out,
        early[:, :hidden_units],
        grad_b_up,
        early[:, hidden_units:].T,
    )


def solution(mesh):
    return jax.shard_map(
        shards,
        mesh=mesh,
        in_specs=(
            P(None, "dp", None),
            P(None, "dp", None),
            P(),
            P(),
            P(),
            P(),
            P(),
            P("dp", "tensor", None),
            P("tensor", None),
            P("tensor", None, "dp"),
            P(),
            P("dp", "tensor"),
            P("tensor"),
            P("tensor", "dp"),
        ),
        out_specs=(
            P(None, "dp", None),
            P(None, "dp", None),
            P(),
            P(),
            P(),
            P(),
            P("dp", "tensor", None),
            P("tensor", None),
            P("tensor", None, "dp"),
            P(),
            P("dp", "tensor"),
            P("tensor"),
            P("tensor", "dp"),
        ),
        check_vma=False,
    )
```

time: 869 us -> 741 us (0.85); the launches traced: 856 us -> 738 us
  waiting for transfers between devices: 368 us -> 315 us
  local copies, waits for them, and re-layouts: 121 us -> 79.5 us
  blocking collectives: 77.1 us -> 42.5 us
    all_to_all x3, waiting for transfers between devices: 137 us -> 70.9 us  [the longest x2 57.6 us: from_units(): array = lax.all_to_all(array, 'dp', split_axis=0, concat_axis=0, tiled=True)]
    psum x1, waiting for transfers between devices: 13.3 us -> 62.2 us  [shards(): grad_unit = lax.psum(grad_unit, 'tensor').astype(jnp.float32)]
    psum x1, waiting for transfers between devices: 69.6 us -> 23.1 us  [shards(): lax.psum((mul(attended, w_out, NT) + down).astype(jnp.bfloat16), 'tensor')]
    pallas_call x2 -> x0, local copies, waits for them, and re-layouts: 45 us -> none  [the longest x1 27.2 us: attention(): pl.pallas_call(partial(attend_back_kernel, rows), grid_spec=pltpu.Prefetc...]
    psum x2 -> x1, blocking collectives: 77.1 us -> 42.5 us  [shards(): sums = lax.psum(sums.reshape(-1, 128), ('dp', 'tensor')).reshape(-1)]
    all_gather x1, waiting for transfers between devices: 0.02 us -> 21.2 us  [shards(): lax.all_gather(jnp.concatenate([fc1_weight, fc2_weight.T], axis=1), 'dp',...]
    reduce_scatter x1 -> x0, waiting for transfers between devices: 9.72 us -> none  [shards(): lax.psum_scatter(mul(first_low, grad_proj, TN).astype(jnp.bfloat16), 'dp'...]
    unnamed x7 -> x8, waiting for transfers between devices: 96.4 us -> 102 us
  transfers between devices with their start and end apart: 9 -> 9, of which waited for: 6 -> 8; matrix products, arithmetic and copies ran while one was open for 22% -> 28% of each run, Pallas kernels for 8% -> 6%
where the time goes in v2:
time: 741 us; the launch traced here: 738 us
  waiting for transfers between devices  315 us (43%)
  matrix products  101 us (14%)
  local copies, waits for them, and re-layouts  79.5 us (11%)
  Pallas kernels  79.5 us (11%)
  starting transfers between devices  57.2 us (8%)
  other arithmetic  48 us (6%)
  blocking collectives  42.5 us (6%)
  between operations  15.3 us (2%)
    unnamed x8, waiting for transfers between devices  102 us
    dot_general x12, matrix products, mul(): return lax.dot_general(a, b, dims, preferred_element_type=jnp.float32)  101 us
    psum x1, waiting for transfers between devices, shards(): grad_unit = lax.psum(grad_unit, 'tensor').astype(jnp.float32)  62.2 us
    all_to_all x2, waiting for transfers between devices, from_units(): array = lax.all_to_all(array, 'dp', split_axis=0, concat_axis=0, tiled=True)  57.6 us
    all_to_all x2, starting transfers between devices, from_units(): array = lax.all_to_all(array, 'dp', split_axis=0, concat_axis=0, tiled=True)  51.9 us
    pallas_call x1, Pallas kernels, attention(): pl.pallas_call(partial(attend_back_kernel, units), grid_spec=pltpu.Prefet...  45.4 us
    psum x1, blocking collectives, shards(): sums = lax.psum(sums.reshape(-1, 128), ('dp', 'tensor')).reshape(-1)  42.5 us
    all_gather x1, waiting for transfers between devices, shards(): lax.all_gather(jnp.concatenate([qkv_weight.reshape(shard_rows, qkv_wide),...  35.6 us
  transfers between devices with their start and end apart: 9, of which 8 were waited for; matrix products, arithmetic and copies ran while one was open for 28% of the time, Pallas kernels for 6%

profile of v2, /device:TPU:0, one launch (start us, length us, event | category | flops | bytes accessed | tf_op | source)
XLA Modules:
  0.0 737.7 jit_solution(9548008273890072075)
XLA Ops:
  7.3 1.7 pad_maximum_fusion.3
  9.0 1.1 copy.92
  10.2 1.8 pad_maximum_fusion.2
  12.9 1.2 gather_fusion
  14.9 2.8 convert_reduce_fusion.1
  17.7 3.0 fusion.15
  21.8 1.0 fusion.54
  22.8 6.1 fusion.28
  28.9 35.6 %all-gather.3.cloned.1.call-done = bf16[1024,1024]{0,1:T(8,128)(2,1)} async-done(((bf16[128,1024]{0,1:T(8,128)(2,1)}), bf16[1024,1024]{0,1:T(8,128)(2,1)}) %all-gather.3.cloned.1.call-update) | async-done | bytes 2097168 | tf_op jit(solution)/shard_map/all_gather | solution.py:226
  64.5 5.7 convolution_add_fusion
  71.9 2.5 copy.87
  74.4 2.5 copy.83
  77.0 1.7 copy.84
  78.7 1.7 copy.86
  80.4 1.0 slice.176
  81.5 1.3 fusion.62
  82.7 2.7 copy.88
  85.4 2.7 copy.85
  88.1 2.9 copy.89
  91.0 4.6 fusion.38
  95.6 1.8 concatenate.56
  97.5 2.5 copy.90
  100.0 17.3 %concatenate.57 = bf16[4,512,4,256]{3,1,0,2:T(8,128)(2,1)} concatenate(bf16[4,512,4,8]{3,1,0,2:T(8,128)(2,1)} %bitcast.168, bf16[4,512,4,8]{3,1,0,2:T(8,128)(2,1)} %bitcast.169, bf16[4,512,4,48]{3,1,0,2:T(8,128)(2,1)} %bitcast.172, bf16[4,512,4,8]{3,1,0,2:T(8,128)(2,1)} %bitcast.170, bf16[4,512,4,8]{3,1,0,2:T(8,128)(2,1)S(1)} %bitcast.167, bf16[4,512,4,48]{3,1,0,2:T(8,128)(2,1)} %bitcast.171, ...), dimensions={3} | concatenate | bytes 8388608 | tf_op jit(solution)/shard_map/concatenate | solution.py:276
  117.3 4.5 copy.104
  121.8 5.0 all-to-all-start
  126.8 21.2 %all-gather.5.cloned.1.call-done = bf16[1024,2048]{0,1:T(8,128)(2,1)} async-done(((bf16[128,2048]{0,1:T(8,128)(2,1)}), bf16[1024,2048]{0,1:T(8,128)(2,1)}) %all-gather.5.cloned.1.call-update) | async-done | bytes 4194320 | tf_op jit(solution)/shard_map/all_gather | solution.py:236
  148.1 26.1 %multiply_convert_fusion = (bf16[2048,1024]{1,0:T(8,128)(2,1)S(1)}, f32[2048,1024]{1,0:T(8,128)}, f32[2048,1024]{1,0:T(8,128)}) fusion(f32[1024]{0:T(1024)S(1)} %copy-done.29, bf16[2048,1024]{1,0:T(8,128)(2,1)} %get-tuple-element.111, bf16[1024,2048]{0,1:T(8,128)(2,1)} %all-gather.5.cloned.1.call-done), kind=kOutput, calls=%fused_computation.48 | convolution fusion | flops 4433379328 | bytes 27267072 | tf_op jit(solution)/shard_map/dot_general | solution.py:56
  174.2 13.2 %convert_reduce_fusion.2 = (f32[1024]{0:T(1024)S(1)}, bf16[2048,1024]{1,0:T(8,128)(2,1)}) fusion(f32[2048,1024]{1,0:T(8,128)} %get-tuple-element.105, bf16[2048,1024]{1,0:T(8,128)(2,1)S(1)} %bitcast.159, bf16[1024,2048]{0,1:T(8,128)(2,1)S(1)} %copy-done.28, f32[2048,1024]{1,0:T(8,128)} %get-tuple-element.130, f32[1024]{0:T(1024)S(1)} %copy-done.29), kind=kOutput, calls=%fused_computation.44 | convolution fusion | flops 4330617856 | bytes 27271168 | tf_op jit(solution)/shard_map/dot_general | solution.py:56
  187.4 7.2 convolution_convert_fusion.1
  194.5 4.8 convert_bitcast_fusion
  199.3 2.6 pad_maximum_fusion
  201.9 1.1 copy-done.31
  203.0 6.9 fusion.42
  209.9 6.9 fusion.39
  216.8 13.3 %all-to-all-done.x_ref = bf16[8,512,512]{2,1,0:T(8,128)(2,1)} async-done(((bf16[8,512,512]{2,1,0:T(8,128)(2,1)}), bf16[8,512,512]{2,1,0:T(8,128)(2,1)}, u32[]{:S(2)}, u32[]{:S(2)}) %all-to-all-start) | async-done | bytes 4194336 | tf_op jit(solution)/shard_map/all_to_all | solution.py:261
  230.1 34.1 %shard_map.237 = (bf16[8,512,128]{2,1,0:T(8,128)(2,1)}, f32[2,1,4096]{2,1,0:T(1,128)S(1)}, f32[2,1,4096]{2,1,0:T(1,128)S(1)}) custom-call(s32[2,8]{1,0:T(2,128)S(1)} %and_select_fusion.first_ref, bf16[8,512,512]{2,1,0:T(8,128)(2,1)} %all-to-all-done.x_ref, s32[2,1,4096]{2,1,0:T(1,128)S(1)} %broadcast_in_dim.47.start_ref), custom_call_target="tpu_custom_call" | custom-call | flops 8589934592 | bytes 5734400 | tf_op jit(solution)/shard_map/pallas_call | solution.py:160
  264.2 24.6 %all-to-all-start.2 = ((bf16[8,512,128]{2,1,0:T(8,128)(2,1)}), bf16[8,512,128]{2,1,0:T(8,128)(2,1)S(1)}, u32[]{:S(2)}, u32[]{:S(2)}) async-start(bf16[8,512,128]{2,1,0:T(8,128)(2,1)} %get-tuple-element.26), calls=%async_computation.2 | async-start | bytes 2097152 | tf_op jit(solution)/shard_map/all_to_all | solution.py:265
  288.8 45.4 %shard_map.238 = bf16[8,512,384]{2,1,0:T(8,128)(2,1)} custom-call(s32[2,8]{1,0:T(2,128)S(1)} %and_select_fusion.1.last_ref, bf16[8,512,512]{2,1,0:T(8,128)(2,1)} %all-to-all-done.x_ref, s32[2,1,4096]{2,1,0:T(1,128)S(1)} %broadcast_in_dim.47.start_ref, f32[2,1,4096]{2,1,0:T(1,128)S(1)} %get-tuple-element.23.lse_ref, f32[2,1,4096]{2,1,0:T(1,128)S(1)} %get-tuple-element.24.delta_ref), custom_call_target="tpu_custom_call" | custom-call | flops 21474836480 | bytes 8192000 | tf_op jit(solution)/shard_map/pallas_call | solution.py:182
  334.2 1.0 copy-done.6
  335.2 27.3 %all-to-all-start.1 = ((bf16[8,512,384]{2,1,0:T(8,128)(2,1)}), bf16[8,512,384]{2,1,0:T(8,128)(2,1)S(1)}, u32[]{:S(2)}, u32[]{:S(2)}) async-start(bf16[8,512,384]{2,1,0:T(8,128)(2,1)} %shard_map.238), calls=%async_computation.1 | async-start | bytes 6291456 | tf_op jit(solution)/shard_map/all_to_all | solution.py:265
  362.5 2.3 copy.96
  364.8 2.0 copy.97
  367.1 1.0 copy-done.4
  368.1 6.9 add_convert_fusion
  375.1 57.6 %all-to-all-done.1 = bf16[8,512,384]{2,1,0:T(8,128)(2,1)S(1)} async-done(((bf16[8,512,384]{2,1,0:T(8,128)(2,1)}), bf16[8,512,384]{2,1,0:T(8,128)(2,1)S(1)}, u32[]{:S(2)}, u32[]{:S(2)}) %all-to-all-start.1) | async-done | bytes 3145760 | tf_op jit(solution)/shard_map/all_to_all | solution.py:265
  432.8 2.9 copy.94
  435.6 2.4 copy.105
  439.1 23.1 %all-reduce.3.cloned.1.call-done = bf16[2048,1024]{1,0:T(8,128)(2,1)} async-done(((bf16[2048,1024]{1,0:T(8,128)(2,1)}), bf16[2048,1024]{1,0:T(8,128)(2,1)}) %all-reduce.3.cloned.1.call-update) | async-done | bytes 4194320 | tf_op jit(solution)/shard_map/psum | solution.py:310
  462.2 14.3 %fusion.59 = (f32[1024]{0:T(1024)S(1)}, f32[1024]{0:T(1024)S(1)}, bf16[2048,1024]{1,0:T(8,128)(2,1)}, bf16[2048,1024]{1,0:T(8,128)(2,1)}, f32[2048,1024]{1,0:T(8,128)}) fusion(f32[2048,1024]{1,0:T(8,128)} %fusion.42, f32[2048]{0:T(1024)S(1)} %bitcast.186, f32[2048]{0:T(1024)S(1)} %bitcast.190, bf16[4,512,1024]{2,1,0:T(8,128)(2,1)} %param.14, ...), kind=kOutput, calls=%fused_computation.148 | convolution fusion | flops 3250583552 | bytes 38309888 | tf_op jit(solution)/shard_map/dot_general | solution.py:56
  476.6 6.5 copy.102
  483.2 3.0 convert_reduce_fusion.3
  486.3 3.7 fusion.18
  490.0 1.2 fusion.49
  491.3 3.4 convolution_convert_fusion.2
  494.9 2.6 copy.100
  497.5 2.4 convert_reduce_fusion.4
  500.1 62.2 %all-reduce.5.cloned.1.call-done = bf16[2048,1024]{1,0:T(8,128)(2,1)} async-done(((bf16[2048,1024]{1,0:T(8,128)(2,1)}), bf16[2048,1024]{1,0:T(8,128)(2,1)}) %all-reduce.5.cloned.1.call-update) | async-done | bytes 4194320 | tf_op jit(solution)/shard_map/psum | solution.py:329
  562.3 7.7 %fusion.60 = (f32[1024]{0:T(1024)S(1)}, f32[1024]{0:T(1024)S(1)}, f32[2048]{0:T(1024)S(1)}, f32[2048]{0:T(1024)S(1)}) fusion(f32[2048,1024]{1,0:T(8,128)} %get-tuple-element.131, f32[2048]{0:T(1024)S(1)} %bitcast.187, f32[2048]{0:T(1024)S(1)} %bitcast.191, bf16[4,512,1024]{2,1,0:T(8,128)(2,1)} %param.14, bf16[2048,1024]{1,0:T(8,128)(2,1)} %all-reduce.5.cloned.1.call-done), kind=kLoop, calls=%fused_computation.149 | loop fusion | flops 20965376 | bytes 16818176 | tf_op jit(solution)/shard_map/reduce_sum | solution.py:357
  570.1 42.5 %psum.23 = f32[96,128]{1,0:T(8,128)S(1)} all-reduce(f32[96,128]{1,0:T(8,128)S(1)} %bitcast.195), channel_id=1, replica_groups=mesh['dp'=8,'tensor'=4] {'dp','tensor'}, use_global_device_ids=true, to_apply=%region_18.19 | all-reduce | flops 12288 | bytes 98304 | tf_op jit(solution)/shard_map/psum | solution.py:364
  614.6 7.6 %fusion.4 = bf16[2048,1024]{1,0:T(8,128)(2,1)} fusion(bf16[2048,1024]{1,0:T(8,128)(2,1)} %all-reduce.5.cloned.1.call-done, bf16[4,512,1024]{2,1,0:T(8,128)(2,1)} %param.14, f32[2048]{0:T(1024)S(1)} %get-tuple-element.134, f32[2048]{0:T(1024)S(1)} %get-tuple-element.135, f32[2048]{0:T(1024)S(1)} %bitcast.188, f32[2048]{0:T(1024)S(1)} %bitcast.192, ...), kind=kLoop, calls=%fused_computation.9 | loop fusion | flops 23068672 | bytes 16809984 | tf_op jit(solution)/shard_map/convert_element_type | solution.py:371
  622.2 33.5 %reduce-scatter.9.cloned.1.call-done = bf16[128,2048]{1,0:T(8,128)(2,1)} async-done(((bf16[1024,2048]{1,0:T(8,128)(2,1)}), bf16[128,2048]{1,0:T(8,128)(2,1)}) %reduce-scatter.9.cloned.1.call-update) | async-done | bytes 524304
  655.7 1.3 copy.103
  657.1 1.0 copy.98
  658.9 68.0 %reduce-scatter.7.cloned.1.call-done = bf16[128,1024]{1,0:T(8,128)(2,1)} async-done(((bf16[1024,1024]{1,0:T(8,128)(2,1)}), bf16[128,1024]{1,0:T(8,128)(2,1)}) %reduce-scatter.7.cloned.1.call-update) | async-done | bytes 262160
  (133 shorter events, 12.8 us)
Async XLA Ops:
  7.2 14.2 %copy-start.27 = (f32[4,192]{1,0:T(4,128)S(1)}, f32[4,192]{1,0:T(4,128)}, u32[]{:S(2)}) copy-start(f32[4,192]{1,0:T(4,128)} %param.22) | copy-start | bytes 9220
  7.2 15.6 %copy-start.22 = (f32[1024]{0:T(1024)S(1)}, f32[1024]{0:T(1024)}, u32[]{:S(2)}) copy-start(f32[1024]{0:T(1024)} %param.17) | copy-start | bytes 12292
  7.2 15.6 %copy-start.20 = (f32[1024]{0:T(1024)S(1)}, f32[1024]{0:T(1024)}, u32[]{:S(2)}) copy-start(f32[1024]{0:T(1024)} %param.18) | copy-start | bytes 12292
  7.2 15.6 %copy-start.25 = (f32[1024]{0:T(1024)S(1)}, f32[1024]{0:T(1024)}, u32[]{:S(2)}) copy-start(f32[1024]{0:T(1024)} %param.19) | copy-start | bytes 12292
  7.2 15.6 %copy-start.24 = (f32[1024]{0:T(1024)S(1)}, f32[1024]{0:T(1024)}, u32[]{:S(2)}) copy-start(f32[1024]{0:T(1024)} %param.20) | copy-start | bytes 12292
  7.2 57.3 %all-gather.3.cloned.1.call-start = ((), (), s32[]{:S(2)}) async-start(), calls=%async_computation.5 | async-start | bytes 2359296 | tf_op jit(solution)/shard_map/all_gather | solution.py:226
  9.0 139.1 %all-gather.5.cloned.1.call-start = ((), (), s32[]{:S(2)}) async-start(), calls=%async_computation.6 | async-start | bytes 4718592 | tf_op jit(solution)/shard_map/all_gather | solution.py:236
  17.7 3.6 copy-start.17
  21.4 48.9 %copy-start.13 = (f32[1,4,4,128]{3,1,2,0:T(4,128)}, f32[1,4,4,128]{3,1,2,0:T(4,128)S(1)}, u32[]{:S(2)}) copy-start(f32[1,4,4,128]{3,1,2,0:T(4,128)S(1)} %copy.107) | copy-start | bytes 24580
  21.4 48.9 %copy-start.15 = (f32[1,4,4,128]{3,1,2,0:T(4,128)}, f32[1,4,4,128]{3,1,2,0:T(4,128)S(1)}, u32[]{:S(2)}) copy-start(f32[1,4,4,128]{3,1,2,0:T(4,128)S(1)} %copy.106) | copy-start | bytes 24580
  22.8 48.0 %copy-start.9 = (f32[2048,8]{0,1:T(8,128)}, f32[2048,8]{0,1:T(8,128)S(1)}, u32[]{:S(2)}) copy-start(f32[2048,8]{0,1:T(8,128)S(1)} %get-tuple-element.125) | copy-start | bytes 196612
  70.2 0.8 copy-start.12
  88.1 11.8 %copy-start.2 = (bf16[2048,4,8]{2,0,1:T(8,128)(2,1)S(1)}, bf16[2048,4,8]{2,0,1:T(8,128)(2,1)}, u32[]{:S(2)}) copy-start(bf16[2048,4,8]{2,0,1:T(8,128)(2,1)} %copy.87) | copy-start | bytes 393220
  117.3 30.8 %copy-start.29 = (f32[1024]{0:T(1024)S(1)}, f32[1024]{0:T(1024)}, u32[]{:S(2)}) copy-start(f32[1024]{0:T(1024)} %param.26) | copy-start | bytes 12292
  121.8 108.3 %all-to-all-start = ((bf16[8,512,512]{2,1,0:T(8,128)(2,1)}), bf16[8,512,512]{2,1,0:T(8,128)(2,1)}, u32[]{:S(2)}, u32[]{:S(2)}) async-start(bf16[8,512,512]{2,1,0:T(8,128)(2,1)} %bitcast.157), calls=%async_computation | async-start | bytes 8388608 | tf_op jit(solution)/shard_map/all_to_all | solution.py:261
  148.1 26.1 %copy-start = (bf16[4,512,1024]{2,1,0:T(8,128)(2,1)S(1)}, bf16[4,512,1024]{2,1,0:T(8,128)(2,1)}, u32[]{:S(2)}) copy-start(bf16[4,512,1024]{2,1,0:T(8,128)(2,1)} %param.15) | copy-start | bytes 12582916
  148.1 26.1 %copy-start.28 = (bf16[1024,2048]{0,1:T(8,128)(2,1)S(1)}, bf16[1024,2048]{0,1:T(8,128)(2,1)}, u32[]{:S(2)}) copy-start(bf16[1024,2048]{0,1:T(8,128)(2,1)} %all-gather.5.cloned.1.call-done) | copy-start | bytes 12582916
  174.2 13.2 %copy-start.3 = (bf16[2048,1024]{1,0:T(8,128)(2,1)S(1)}, bf16[2048,1024]{1,0:T(8,128)(2,1)}, u32[]{:S(2)}) copy-start(bf16[2048,1024]{1,0:T(8,128)(2,1)} %get-tuple-element.111) | copy-start | bytes 12582916
  199.3 3.7 copy-start.31
  264.2 70.0 %all-to-all-start.2 = ((bf16[8,512,128]{2,1,0:T(8,128)(2,1)}), bf16[8,512,128]{2,1,0:T(8,128)(2,1)S(1)}, u32[]{:S(2)}, u32[]{:S(2)}) async-start(bf16[8,512,128]{2,1,0:T(8,128)(2,1)} %get-tuple-element.26), calls=%async_computation.2 | async-start | bytes 2097152 | tf_op jit(solution)/shard_map/all_to_all | solution.py:265
  334.2 1.0 copy-start.6
  335.2 97.6 %all-to-all-start.1 = ((bf16[8,512,384]{2,1,0:T(8,128)(2,1)}), bf16[8,512,384]{2,1,0:T(8,128)(2,1)S(1)}, u32[]{:S(2)}, u32[]{:S(2)}) async-start(bf16[8,512,384]{2,1,0:T(8,128)(2,1)} %shard_map.238), calls=%async_computation.1 | async-start | bytes 6291456 | tf_op jit(solution)/shard_map/all_to_all | solution.py:265
  362.5 99.7 %all-reduce.3.cloned.1.call-start = ((), (), s32[]{:S(2)}) async-start(), calls=%async_computation.7 | async-start | bytes 8388608 | tf_op jit(solution)/shard_map/psum | solution.py:310
  367.1 1.0 copy-start.4
  375.1 63.5 %copy-start.10 = (f32[2048,8]{0,1:T(8,128)S(1)}, f32[2048,8]{0,1:T(8,128)}, u32[]{:S(2)}) copy-start(f32[2048,8]{0,1:T(8,128)} %copy-done.9) | copy-start | bytes 196612
  375.1 63.5 %copy-start.11 = (f32[2048,8]{0,1:T(8,128)S(1)}, f32[2048,8]{0,1:T(8,128)}, u32[]{:S(2)}) copy-start(f32[2048,8]{0,1:T(8,128)} %get-tuple-element.123) | copy-start | bytes 196612
  375.1 187.2 %all-reduce.5.cloned.1.call-start = ((), (), s32[]{:S(2)}) async-start(), calls=%async_computation.8 | async-start | bytes 8388608 | tf_op jit(solution)/shard_map/psum | solution.py:329
  438.0 24.1 %copy-start.14 = (f32[1,4,4,128]{3,1,2,0:T(4,128)S(1)}, f32[1,4,4,128]{3,1,2,0:T(4,128)}, u32[]{:S(2)}) copy-start(f32[1,4,4,128]{3,1,2,0:T(4,128)} %copy-done.13) | copy-start | bytes 24580
  438.0 24.1 %copy-start.16 = (f32[1,4,4,128]{3,1,2,0:T(4,128)S(1)}, f32[1,4,4,128]{3,1,2,0:T(4,128)}, u32[]{:S(2)}) copy-start(f32[1,4,4,128]{3,1,2,0:T(4,128)} %copy-done.15) | copy-start | bytes 24580
  438.0 24.1 %copy-start.23 = (f32[1024]{0:T(1024)S(1)}, f32[1024]{0:T(1024)}, u32[]{:S(2)}) copy-start(f32[1024]{0:T(1024)} %param.17) | copy-start | bytes 12292
  438.0 24.1 %copy-start.26 = (f32[1024]{0:T(1024)S(1)}, f32[1024]{0:T(1024)}, u32[]{:S(2)}) copy-start(f32[1024]{0:T(1024)} %param.19) | copy-start | bytes 12292
  438.0 24.1 %copy-start.30 = (f32[1024]{0:T(1024)S(1)}, f32[1024]{0:T(1024)}, u32[]{:S(2)}) copy-start(f32[1024]{0:T(1024)} %param.24) | copy-start | bytes 12292
  439.1 37.4 %copy-start.7 = (bf16[2048,4,192]{0,2,1:T(8,128)(2,1)}, bf16[2048,4,192]{0,2,1:T(8,128)(2,1)S(1)}, u32[]{:S(2)}) copy-start(bf16[2048,4,192]{0,2,1:T(8,128)(2,1)S(1)} %convert_dynamic-update-slice_fusion) | copy-start | bytes 9437188
  476.5 9.8 %copy-start.18 = (f32[4,512]{1,0:T(4,128)S(1)}, f32[4,512]{1,0:T(4,128)}, u32[]{:S(2)}) copy-start(f32[4,512]{1,0:T(4,128)} %copy-done.17) | copy-start | bytes 24580
  476.5 9.8 %copy-start.19 = (f32[4,512]{1,0:T(4,128)S(1)}, f32[4,512]{1,0:T(4,128)}, u32[]{:S(2)}) copy-start(f32[4,512]{1,0:T(4,128)} %get-tuple-element.126) | copy-start | bytes 24580
  476.5 9.8 %copy-start.21 = (f32[1024]{0:T(1024)S(1)}, f32[1024]{0:T(1024)}, u32[]{:S(2)}) copy-start(f32[1024]{0:T(1024)} %param.18) | copy-start | bytes 12292
  476.5 179.2 %reduce-scatter.9.cloned.1.call-start = ((), (), s32[]{:S(2)}) async-start(), calls=%async_computation.10 | async-start | bytes 4718592
  483.1 6.9 copy-start.5
  483.1 243.8 %reduce-scatter.7.cloned.1.call-start = ((), (), s32[]{:S(2)}) async-start(), calls=%async_computation.9 | async-start | bytes 2359296
  483.2 6.8 copy-start.1
  486.2 5.0 copy-start.8
Sparse Core Ops, SparseCore 0:
  10.7 53.7 all-gather.2
  67.1 80.9 all-gather.4
  375.2 86.9 all-reduce.2
  476.6 85.6 all-reduce.4
  565.7 89.8 reduce-scatter.8
  659.5 67.4 reduce-scatter.6
